TPU v7x, 32 devices: a whole 2x2x4 slice. The times are simulated.
32 devices in a mesh: dp: 16 (over z, y, x), blk: 2 (over core).
Axes of the slice: x: 2, y: 2, z: 4, core: 2. Of those that a mesh axis runs over, the one named last changes fastest.
Arguments:
- tubes: bfloat16 [16, 1024, 768], P('dp', 'blk'), may hold values from -6 to 6
- tube_mask: int32 [16, 1024], P('dp', 'blk'), may hold values 0 or 1
- tube_order: int32 [16, 1024], P('dp', 'blk'), may hold values from 0 to 1023, each once within a row
- cotangent: bfloat16 [16, 1024, 768], P('dp', 'blk'), may hold values from -6 to 6
- mask_token: float32 [768], replicated, may hold values from -6 to 6
- pos_table: bfloat16 [1024, 768], replicated, may hold values from -3 to 3
- ln1_gain: float32 [768], replicated, may hold values from 0.5 to 1.5
- ln1_bias: float32 [768], replicated, may hold values from -3 to 3
- w_qkv: bfloat16 [768, 2304], replicated, may hold values from -0.21875 to 0.21875
- bias_q: float32 [768], replicated, may hold values from -3 to 3
- bias_v: float32 [768], replicated, may hold values from -3 to 3
- w_out: bfloat16 [768, 768], replicated, may hold values from -3.5 to 3.5
- bias_out: float32 [768], replicated, may hold values from -3 to 3
- ln2_gain: float32 [768], replicated, may hold values from 0.5 to 1.5
- ln2_bias: float32 [768], replicated, may hold values from -3 to 3
- w_up: bfloat16 [768, 3072], replicated, may hold values from -0.21875 to 0.21875
- bias_up: float32 [3072], replicated, may hold values from -3 to 3
- w_down: bfloat16 [3072, 768], replicated, may hold values from -0.109375 to 0.109375
- bias_down: float32 [768], replicated, may hold values from -3 to 3
Outputs:
- output: bfloat16 [16, 1024, 768], P('dp', 'blk')
- grad_tubes: float32 [16, 1024, 768], P('dp', 'blk')
- grad_mask_token: float32 [768], P(('dp', 'blk'))
- grad_pos_table: float32 [1024, 768], P(None, ('dp', 'blk'))
- grad_ln1_gain: float32 [768], P(('dp', 'blk'))
- grad_ln1_bias: float32 [768], P(('dp', 'blk'))
- grad_w_qkv: float32 [768, 2304], P(('dp', 'blk'))
- grad_bias_q: float32 [768], P(('dp', 'blk'))
- grad_bias_v: float32 [768], P(('dp', 'blk'))
- grad_w_out: float32 [768, 768], P(('dp', 'blk'))
- grad_bias_out: float32 [768], P(('dp', 'blk'))
- grad_ln2_gain: float32 [768], P(('dp', 'blk'))
- grad_ln2_bias: float32 [768], P(('dp', 'blk'))
- grad_w_up: float32 [768, 3072], P(('dp', 'blk'))
- grad_bias_up: float32 [3072], P(('dp', 'blk'))
- grad_w_down: float32 [3072, 768], P(('dp', 'blk'))
- grad_bias_down: float32 [768], P(('dp', 'blk'))
Inputs may be any that keep to these rules, and one draw needn't show every extreme that they name: `tube_mask`: 1 marks a masked tube. `tube_order`: each clip's row is a permutation of 0 to 1023.
All inputs are finite; a program needn't handle non-finite values. No bound on the sum of `tube_mask` on one device may be relied on, other than what follows from the above.
Results may differ from a plain program's by a relative error of at most 0.019.
Values may be sent and summed in bfloat16 or wider, within the bound.
No kernel may reach another device: no remote copies, remote signals or barrier semaphores. Data moves between devices by JAX's collectives and lax.ppermute only.
A program may use at most 192 MiB of HBM per device.

v0:
```python
import jax
import jax.numpy as jnp
from jax import lax
from jax.sharding import PartitionSpec as P

HEADS = 12
HEAD_DIM = 64


epsilon = 1e-06
score_scale = 0.125


def norm_forward(rows_in, gain_vec, shift_vec):
    row_mean = jnp.mean(rows_in, -1, keepdims=True)
    centered = rows_in - row_mean
    variance = jnp.mean(centered * centered, -1, keepdims=True)
    inverse = lax.rsqrt(variance + epsilon)
    unit_rows = centered * inverse
    return (unit_rows * gain_vec + shift_vec, unit_rows, inverse)


def norm_backward(grad_rows, unit_rows, inverse, gain_vec):
    scaled_grad = grad_rows * gain_vec
    grad_input = inverse * (
        scaled_grad
        - jnp.mean(scaled_grad, -1, keepdims=True)
        - unit_rows * jnp.mean(scaled_grad * unit_rows, -1, keepdims=True)
    )
    return (grad_input, jnp.sum(grad_rows * unit_rows, 0), jnp.sum(grad_rows, 0))


def across(left, right):
    return lax.dot_general(
        left, right, (((0,), (0,)), ((), ())), preferred_element_type=jnp.float32
    )


def against(left, weight):
    return lax.dot_general(
        left, weight, (((1,), (1,)), ((), ())), preferred_element_type=jnp.float32
    )


def activation(pre_act):
    return jax.nn.gelu(pre_act, approximate=False)


def pair_terms(query_part, grad_part, log_part, dot_part, key_heads, value_heads):
    scores = (
        jnp.einsum("cqhd,ckhd->chqk", query_part, key_heads, preferred_element_type=jnp.float32)
        * score_scale
    )
    probabilities = jnp.exp(scores - log_part[..., None])
    grad_probs = jnp.einsum(
        "cqhd,ckhd->chqk", grad_part, value_heads, preferred_element_type=jnp.float32
    )
    grad_scores = (probabilities * (grad_probs - dot_part[..., None])).astype(jnp.bfloat16)
    return (probabilities, grad_scores)


def body(
    tubes,
    tube_mask,
    tube_order,
    cotangent,
    mask_token,
    pos_table,
    ln1_gain,
    ln1_bias,
    w_qkv,
    bias_q,
    bias_v,
    w_out,
    bias_out,
    ln2_gain,
    ln2_bias,
    w_up,
    bias_up,
    w_down,
    bias_down,
):
    clip_count, block_rows, model_width = tubes.shape
    row_total = clip_count * block_rows
    length = block_rows * lax.axis_size("blk")
    masked = (tube_mask == 1)[..., None]
    embedded = jnp.where(masked, mask_token, tubes.astype(jnp.float32)) + pos_table[
        tube_order
    ].astype(jnp.float32)
    embedded_rows = embedded.reshape(row_total, model_width)
    normed_one, unit_one, inverse_one = norm_forward(embedded_rows, ln1_gain, ln1_bias)
    normed_one_low = normed_one.astype(jnp.bfloat16)
    packed = jnp.dot(normed_one_low, w_qkv, preferred_element_type=jnp.float32)
    queries = (
        (packed[:, :model_width] + bias_q)
        .astype(jnp.bfloat16)
        .reshape(clip_count, block_rows, HEADS, HEAD_DIM)
    )
    key_rows = (
        packed[:, model_width : 2 * model_width]
        .astype(jnp.bfloat16)
        .reshape(clip_count, block_rows, model_width)
    )
    values = (
        (packed[:, 2 * model_width :] + bias_v)
        .astype(jnp.bfloat16)
        .reshape(clip_count, block_rows, model_width)
    )
    run_max = jnp.full((clip_count, HEADS, block_rows), -1e30, jnp.float32)
    run_sum = jnp.zeros((clip_count, block_rows, HEADS, HEAD_DIM), jnp.float32)
    key_part = lax.all_gather(key_rows, "blk", axis=1, tiled=True)
    value_part = lax.all_gather(values, "blk", axis=1, tiled=True)
    key_count = key_part.shape[1]
    key_heads = key_part.reshape(clip_count, key_count, HEADS, HEAD_DIM)
    value_heads = value_part.reshape(clip_count, key_count, HEADS, HEAD_DIM)
    scores = (
        jnp.einsum("cqhd,ckhd->chqk", queries, key_heads, preferred_element_type=jnp.float32)
        * score_scale
    )
    new_max = jnp.maximum(run_max, jnp.max(scores, -1))
    shrink = jnp.exp(run_max - new_max)
    weights = jnp.exp(scores - new_max[..., None])
    run_total = jnp.sum(weights, -1)
    run_sum = run_sum * jnp.swapaxes(shrink, 1, 2)[..., None] + jnp.einsum(
        "chqk,ckhd->cqhd",
        weights.astype(jnp.bfloat16),
        value_heads,
        preferred_element_type=jnp.float32,
    )
    run_max, run_total, run_sum = (new_max, run_total, run_sum)
    log_total = run_max + jnp.log(run_total)
    attended_full = (run_sum / jnp.swapaxes(run_total, 1, 2)[..., None]).reshape(
        row_total, model_width
    )
    attended_low = attended_full.astype(jnp.bfloat16)
    after_attn = (
        embedded_rows + jnp.dot(attended_low, w_out, preferred_element_type=jnp.float32) + bias_out
    )
    normed_two, unit_two, inverse_two = norm_forward(after_attn, ln2_gain, ln2_bias)
    normed_two_low = normed_two.astype(jnp.bfloat16)
    pre_act = jnp.dot(normed_two_low, w_up, preferred_element_type=jnp.float32) + bias_up
    active_low = activation(pre_act).astype(jnp.bfloat16)
    result = (
        after_attn + jnp.dot(active_low, w_down, preferred_element_type=jnp.float32) + bias_down
    )
    output = result.astype(jnp.bfloat16).reshape(clip_count, block_rows, model_width)
    cot_rows = cotangent.reshape(row_total, model_width)
    cot_float = cot_rows.astype(jnp.float32)
    grad_w_down = across(active_low, cot_rows)
    grad_bias_down = jnp.sum(cot_float, 0)
    grad_active = against(cot_rows, w_down)
    gelu_out, gelu_pull = jax.vjp(activation, pre_act)
    grad_pre = gelu_pull(grad_active)[0].astype(jnp.bfloat16)
    grad_w_up = across(normed_two_low, grad_pre)
    grad_bias_up = jnp.sum(grad_pre.astype(jnp.float32), 0)
    grad_normed_two = against(grad_pre, w_up)
    grad_mid, grad_ln2_gain, grad_ln2_bias = norm_backward(
        grad_normed_two, unit_two, inverse_two, ln2_gain
    )
    grad_after = cot_float + grad_mid
    grad_branch = grad_after.astype(jnp.bfloat16)
    grad_w_out = across(attended_low, grad_branch)
    grad_bias_out = jnp.sum(grad_branch.astype(jnp.float32), 0)
    grad_attended = against(grad_branch, w_out)
    grad_att_heads = grad_attended.astype(jnp.bfloat16).reshape(
        clip_count, block_rows, HEADS, HEAD_DIM
    )
    row_dot = jnp.swapaxes(
        jnp.sum(
            grad_att_heads.astype(jnp.float32)
            * attended_full.reshape(clip_count, block_rows, HEADS, HEAD_DIM),
            -1,
        ),
        1,
        2,
    )
    key_part = lax.all_gather(key_rows, "blk", axis=1, tiled=True)
    value_part = lax.all_gather(values, "blk", axis=1, tiled=True)
    key_count = key_part.shape[1]
    key_heads = key_part.reshape(clip_count, key_count, HEADS, HEAD_DIM)
    value_heads = value_part.reshape(clip_count, key_count, HEADS, HEAD_DIM)
    probabilities, grad_scores = pair_terms(
        queries, grad_att_heads, log_total, row_dot, key_heads, value_heads
    )
    grad_query = (
        jnp.einsum("chqk,ckhd->cqhd", grad_scores, key_heads, preferred_element_type=jnp.float32)
        * score_scale
    )
    grad_key = (
        jnp.einsum("chqk,cqhd->ckhd", grad_scores, queries, preferred_element_type=jnp.float32)
        * score_scale
    )
    grad_value = jnp.einsum(
        "chqk,cqhd->ckhd",
        probabilities.astype(jnp.bfloat16),
        grad_att_heads,
        preferred_element_type=jnp.float32,
    )
    grad_block = jnp.concatenate(
        [
            grad_key.reshape(clip_count, key_count, model_width),
            grad_value.reshape(clip_count, key_count, model_width),
        ],
        -1,
    )
    key_terms = grad_block
    outcome = (grad_query, key_terms)
    grad_query, key_terms = outcome
    key_value_grad = lax.psum_scatter(
        key_terms.astype(jnp.bfloat16), "blk", scatter_dimension=1, tiled=True
    ).astype(jnp.float32)
    grad_packed = jnp.concatenate(
        [
            grad_query.reshape(row_total, model_width),
            key_value_grad.reshape(row_total, 2 * model_width),
        ],
        -1,
    ).astype(jnp.bfloat16)
    grad_w_qkv = across(normed_one_low, grad_packed)
    column_sums = jnp.sum(grad_packed.astype(jnp.float32), 0)
    grad_bias_q = column_sums[:model_width]
    grad_bias_v = column_sums[2 * model_width :]
    grad_normed_one = against(grad_packed, w_qkv)
    grad_low, grad_ln1_gain, grad_ln1_bias = norm_backward(
        grad_normed_one, unit_one, inverse_one, ln1_gain
    )
    grad_embedded = grad_after + grad_low
    grad_cube = grad_embedded.reshape(clip_count, block_rows, model_width)
    grad_tubes = jnp.where(masked, 0.0, grad_cube)
    grad_mask_token = jnp.sum(jnp.where(masked, grad_cube, 0.0), (0, 1))
    grad_pos_table = jax.ops.segment_sum(
        grad_embedded, tube_order.reshape(row_total), num_segments=length
    )
    (
        grad_mask_token,
        grad_pos_table,
        grad_ln1_gain,
        grad_ln1_bias,
        grad_w_qkv,
        grad_bias_q,
        grad_bias_v,
        grad_w_out,
        grad_bias_out,
        grad_ln2_gain,
        grad_ln2_bias,
        grad_w_up,
        grad_bias_up,
        grad_w_down,
        grad_bias_down,
    ) = (
        lax.psum_scatter(grad_mask_token, ("dp", "blk"), scatter_dimension=0, tiled=True),
        lax.psum_scatter(grad_pos_table, ("dp", "blk"), scatter_dimension=1, tiled=True),
        lax.psum_scatter(grad_ln1_gain, ("dp", "blk"), scatter_dimension=0, tiled=True),
        lax.psum_scatter(grad_ln1_bias, ("dp", "blk"), scatter_dimension=0, tiled=True),
        lax.psum_scatter(grad_w_qkv, ("dp", "blk"), scatter_dimension=0, tiled=True),
        lax.psum_scatter(grad_bias_q, ("dp", "blk"), scatter_dimension=0, tiled=True),
        lax.psum_scatter(grad_bias_v, ("dp", "blk"), scatter_dimension=0, tiled=True),
        lax.psum_scatter(grad_w_out, ("dp", "blk"), scatter_dimension=0, tiled=True),
        lax.psum_scatter(grad_bias_out, ("dp", "blk"), scatter_dimension=0, tiled=True),
        lax.psum_scatter(grad_ln2_gain, ("dp", "blk"), scatter_dimension=0, tiled=True),
        lax.psum_scatter(grad_ln2_bias, ("dp", "blk"), scatter_dimension=0, tiled=True),
        lax.psum_scatter(grad_w_up, ("dp", "blk"), scatter_dimension=0, tiled=True),
        lax.psum_scatter(grad_bias_up, ("dp", "blk"), scatter_dimension=0, tiled=True),
        lax.psum_scatter(grad_w_down, ("dp", "blk"), scatter_dimension=0, tiled=True),
        lax.psum_scatter(grad_bias_down, ("dp", "blk"), scatter_dimension=0, tiled=True),
    )
    return (
        output,
        grad_tubes,
        grad_mask_token,
        grad_pos_table,
        grad_ln1_gain,
        grad_ln1_bias,
        grad_w_qkv,
        grad_bias_q,
        grad_bias_v,
        grad_w_out,
        grad_bias_out,
        grad_ln2_gain,
        grad_ln2_bias,
        grad_w_up,
        grad_bias_up,
        grad_w_down,
        grad_bias_down,
    )


def solution(mesh):
    in_specs = (
        P("dp", "blk", None),
        P("dp", "blk"),
        P("dp", "blk"),
        P("dp", "blk", None),
        P(),
        P(),
        P(),
        P(),
        P(),
        P(),
        P(),
        P(),
        P(),
        P(),
        P(),
        P(),
        P(),
        P(),
        P(),
    )
    out_specs = (
        P("dp", "blk", None),
        P("dp", "blk", None),
        P(("dp", "blk")),
        P(None, ("dp", "blk")),
        P(("dp", "blk")),
        P(("dp", "blk")),
        P(("dp", "blk"), None),
        P(("dp", "blk")),
        P(("dp", "blk")),
        P(("dp", "blk"), None),
        P(("dp", "blk")),
        P(("dp", "blk")),
        P(("dp", "blk")),
        P(("dp", "blk"), None),
        P(("dp", "blk")),
        P(("dp", "blk"), None),
        P(("dp", "blk")),
    )
    return jax.shard_map(body, mesh=mesh, in_specs=in_specs, out_specs=out_specs, check_vma=False)
```

profile of v0, /device:TPU:0, one launch (start us, length us, event | category | flops | bytes accessed | tf_op | source)
XLA Modules:
  0.0 806.1 jit_solution(5117074024783403214)
XLA Ops:
  7.2 0.9 compare_reduce_fusion
  8.1 0.9 compare_select_fusion
  9.0 4.7 gather_fusion
  13.7 1.9 fusion.46
  15.7 2.0 multiply_reduce_fusion.7
  17.7 2.4 fusion.43
  20.1 2.1 copy-done.12
  22.2 1.0 slice.35
  23.3 3.3 fusion.19
  26.8 2.3 copy.51
  29.1 6.8 all-gather.5.cloned.1.call-done
  35.9 2.6 copy.52
  38.5 14.2 %multiply_reduce_fusion = (f32[12,512]{1,0:T(8,128)S(1)}, f32[12,512,1024]{2,1,0:T(8,128)}) fusion(bf16[512,12,64]{0,2,1:T(8,128)(2,1)} %bitcast.135, bf16[1024,12,64]{0,2,1:T(8,128)(2,1)} %bitcast.132), kind=kOutput, calls=%fused_computation.8 | convolution fusion | flops 817883136 | bytes 27549696 | tf_op jit(solution)/shard_map/cqhd,ckhd->chqk/dot_general | solution.py:117
  52.7 11.0 %fusion = f32[12,512]{1,0:T(8,128)S(1)} fusion(f32[12,512,1024]{2,1,0:T(8,128)} %get-tuple-element.83, f32[12,512]{1,0:T(8,128)S(1)} %broadcast_maximum_fusion), kind=kLoop, calls=%fused_computation.5 | loop fusion | flops 18868224 | bytes 25214976 | tf_op jit(solution)/shard_map/reduce_sum | solution.py:123
  63.7 0.6 copy-done.19
  64.3 0.6 log_add_fusion
  64.9 2.6 copy.53
  67.5 12.5 %fusion.49 = (bf16[1,512,12,64]{1,3,2,0:T(8,128)(2,1)S(1)}, f32[1,512,12,64]{1,3,2,0:T(8,128)}) fusion(f32[512,12]{0,1:T(8,128)} %bitcast.150, bf16[1024,12,64]{0,2,1:T(8,128)(2,1)} %bitcast.130, f32[12,512,1024]{2,1,0:T(8,128)} %get-tuple-element.83, f32[12,512]{1,0:T(8,128)} %copy-done.18, f32[512,12]{0,1:T(8,128)} %get-tuple-element.79), kind=kOutput, calls=%fused_computation.104 | convolution fusion | flops 825360384 | bytes 29171712 | tf_op jit(solution)/shard_map/chqk,ckhd->cqhd/dot_general | solution.py:124
  80.1 1.0 fusion.50
  81.2 0.3 multiply_reduce_fusion.6
  81.5 20.7 %multiply_convert_fusion.1 = (bf16[512,3072]{1,0:T(8,128)(2,1)}, f32[512,3072]{1,0:T(8,128)}, f32[512,3072]{1,0:T(8,128)}) fusion(f32[3072]{0:T(1024)S(1)} %copy-done.32, bf16[768,3072]{1,0:T(8,128)(2,1)} %param.34, f32[512,768]{1,0:T(8,128)S(1)} %get-tuple-element.87, f32[768]{0:T(1024)S(1)} %copy-done.34, f32[768]{0:T(1024)S(1)} %copy-done.28, ...), kind=kOutput, calls=%fused_computation.17 | convolution fusion | flops 2521694208 | bytes 22042624 | tf_op jit(solution)/shard_map/dot_general | solution.py:141
  102.2 9.4 %convert_reduce_fusion = (f32[3072]{0:T(1024)}, bf16[512,3072]{1,0:T(8,128)(2,1)}) fusion(f32[512,3072]{1,0:T(8,128)} %get-tuple-element.74, bf16[3072,768]{1,0:T(8,128)(2,1)S(1)} %bitcast.157, bf16[1,512,768]{2,1,0:T(8,128)(2,1)S(1)} %copy-done.16, f32[512,3072]{1,0:T(8,128)} %get-tuple-element.88, f32[3072]{0:T(1024)S(1)} %copy-done.32), kind=kOutput, calls=%fused_computation.15 | convolution fusion | flops 2442654720 | bytes 21258240 | tf_op jit(solution)/shard_map/dot_general | solution.py:40
  111.6 5.5 multiply_reduce_fusion.1
  117.1 1.3 convert_reduce_fusion.3
  118.5 1.1 copy-done.1
  119.6 1.7 convolution_convert_fusion
  121.3 2.6 copy.55
  124.0 2.3 copy.54
  126.3 3.0 multiply_reduce_fusion.4
  129.3 12.3 %fusion.15 = bf16[12,64,1024]{2,1,0:T(8,128)(2,1)} fusion(bf16[512,12,64]{0,2,1:T(8,128)(2,1)S(1)} %bitcast.139, f32[12,512,1024]{2,1,0:T(8,128)} %get-tuple-element.83, f32[12,512]{1,0:T(8,128)S(1)} %copy-done.17), kind=kOutput, calls=%fused_computation.37 | convolution fusion | flops 824967168 | bytes 27549696 | tf_op jit(solution)/shard_map/chqk,cqhd->ckhd/dot_general | solution.py:193
  141.6 15.2 %multiply_convert_fusion = bf16[12,512,1024]{2,1,0:T(8,128)(2,1)} fusion(f32[12,512,1024]{2,1,0:T(8,128)} %get-tuple-element.83, f32[12,512]{1,0:T(8,128)} %bitcast.151, f32[12,512]{1,0:T(8,128)} %get-tuple-element.78, bf16[512,12,64]{0,2,1:T(8,128)(2,1)} %bitcast.138, bf16[1024,12,64]{0,2,1:T(8,128)(2,1)} %bitcast.131), kind=kOutput, calls=%fused_computation.2 | convolution fusion | flops 836763648 | bytes 40157184 | tf_op jit(solution)/shard_map/cqhd,ckhd->chqk/dot_general | solution.py:55
  156.7 7.2 multiply_convert_fusion.2
  164.0 2.0 pad_maximum_fusion
  166.0 3.8 fusion.38
  169.9 0.2 reduce-scatter.19.cloned.1.call-start
  170.1 11.0 %multiply_convert_fusion.3 = bf16[12,64,512]{2,1,0:T(8,128)(2,1)} fusion(bf16[1024,12,64]{0,2,1:T(8,128)(2,1)} %bitcast.133, bf16[12,512,1024]{2,1,0:T(8,128)(2,1)} %multiply_convert_fusion), kind=kOutput, calls=%fused_computation.58 | convolution fusion | flops 806092800 | bytes 14942208 | tf_op jit(solution)/shard_map/chqk,ckhd->cqhd/dot_general | solution.py:186
  181.1 5.6 multiply_reduce_fusion.2
  186.8 2.5 select_reduce_fusion
  189.3 6.5 scatter_custom_fusion
  195.8 3.6 copy.57
  199.4 0.3 reduce-scatter.15.cloned.1.call-start
  199.6 9.0 %fusion.44 = f32[768,3072]{1,0:T(8,128)} fusion(bf16[512,3072]{1,0:T(8,128)(2,1)} %get-tuple-element.92, f32[512,768]{1,0:T(8,128)} %copy-done.10, f32[768]{0:T(1024)} %param.33, f32[768]{0:T(1024)} %param.32, f32[512]{0:T(512)} %copy-done.27, f32[512]{0:T(512)S(1)} %broadcast_multiply_fusion.4), kind=kOutput, calls=%fused_computation.100 | convolution fusion | flops 2417885184 | bytes 14166016 | tf_op jit(solution)/shard_map/dot_general | solution.py:34
  208.7 8.4 %fusion.28 = f32[3072,768]{1,0:T(8,128)} fusion(bf16[512,3072]{1,0:T(8,128)(2,1)} %get-tuple-element.73, bf16[1,512,768]{2,1,0:T(8,128)(2,1)} %param.22), kind=kOutput, calls=%fused_computation.72 | convolution fusion | flops 2415919104 | bytes 13369344 | tf_op jit(solution)/shard_map/dot_general | solution.py:34
  217.2 0.6 copy-done.26
  217.8 7.6 fusion.34
  225.5 7.4 fusion.27
  232.9 0.4 convert_reduce_fusion.1
  233.3 0.6 fusion.48
  233.9 42.6 %all-reduce.10 = (f32[768]{0:T(1024)}, f32[768]{0:T(1024)}, f32[768]{0:T(1024)}, f32[768]{0:T(1024)}, f32[768]{0:T(1024)}, /*index=5*/f32[768]{0:T(1024)}, f32[7...) all-reduce(f32[768]{0:T(1024)S(1)} %copy-done.23, ...), channel_id=5, replica_groups=mesh['dp'=16,'blk'=2] {'dp','blk'}, use_global_device_ids=true, to_apply=%region_13.14.clone | all-reduce | flops 9984 | bytes 79872
  276.5 1.3 dynamic-slice
  277.8 1.3 dynamic-slice.1
  279.0 1.3 dynamic-slice.2
  280.3 1.2 dynamic-slice.3
  281.5 1.3 dynamic-slice.4
  282.8 1.3 dynamic-slice.5
  284.0 1.3 dynamic-slice.6
  285.3 1.3 dynamic-slice.7
  286.6 1.3 dynamic-slice.9
  287.8 1.3 dynamic-slice.8
  289.1 2.7 select_bitcast_fusion
  291.8 99.6 %reduce-scatter.19.cloned.1.call-done = f32[24,1024]{1,0:T(8,128)} async-done(((f32[768,1024]{1,0:T(8,128)}), f32[24,1024]{1,0:T(8,128)}) %reduce-scatter.19.cloned.1.call-update) | async-done | bytes 98320
  391.4 141.0 %reduce-scatter.15.cloned.1.call-done = f32[24,3072]{1,0:T(8,128)} async-done(((f32[768,3072]{1,0:T(8,128)}), f32[24,3072]{1,0:T(8,128)}) %reduce-scatter.15.cloned.1.call-update) | async-done | bytes 294928 | tf_op jit(solution)/shard_map/reduce_scatter | solution.py:262
  532.5 142.1 %reduce-scatter.17.cloned.1.call-done = f32[96,768]{1,0:T(8,128)} async-done(((f32[3072,768]{1,0:T(8,128)}), f32[96,768]{1,0:T(8,128)}) %reduce-scatter.17.cloned.1.call-update) | async-done | bytes 294928 | tf_op jit(solution)/shard_map/reduce_scatter | solution.py:264
  674.6 124.4 %reduce-scatter.11.cloned.1.call-done = f32[24,2304]{1,0:T(8,128)} async-done(((f32[768,2304]{1,0:T(8,128)}), f32[24,2304]{1,0:T(8,128)}) %reduce-scatter.11.cloned.1.call-update) | async-done | bytes 221200 | tf_op jit(solution)/shard_map/reduce_scatter | solution.py:255
  (104 shorter events, 0.8 us)
Async XLA Ops:
  7.2 10.5 %copy-start = (bf16[768,2304]{1,0:T(8,128)(2,1)S(1)}, bf16[768,2304]{1,0:T(8,128)(2,1)}, u32[]{:S(2)}) copy-start(bf16[768,2304]{1,0:T(8,128)(2,1)} %param.27) | copy-start | bytes 10616836
  7.2 28.7 %all-gather.5.cloned.1.call-start = ((), (), s32[]{:S(2)}) async-start(), calls=%async_computation.11 | async-start | bytes 2359296 | tf_op jit(solution)/shard_map/all_gather | solution.py:111
  9.0 4.7 copy-start.20
  13.7 4.0 copy-start.3
  13.7 4.0 copy-start.6
  13.7 4.0 copy-start.29
  13.7 4.0 copy-start.35
  17.7 2.4 copy-start.24
  20.1 2.1 copy-start.12
  23.2 41.7 %all-gather.7.cloned.1.call-start = ((), (), s32[]{:S(2)}) async-start(), calls=%async_computation.12 | async-start | bytes 2359296 | tf_op jit(solution)/shard_map/all_gather | solution.py:112
  26.6 154.5 %reduce-scatter.9.cloned.1.call-start = ((), (), s32[]{:S(2)}) async-start(), calls=%async_computation.6 | async-start | bytes 4718592 | tf_op jit(solution)/shard_map/reduce_scatter | solution.py:209
  52.7 11.0 %copy-start.18 = (f32[12,512]{1,0:T(8,128)}, f32[12,512]{1,0:T(8,128)S(1)}, u32[]{:S(2)}) copy-start(f32[12,512]{1,0:T(8,128)S(1)} %broadcast_maximum_fusion) | copy-start | bytes 73732
  63.7 0.6 copy-start.19
  67.5 12.5 %copy-start.4 = (bf16[512,768]{1,0:T(8,128)(2,1)S(1)}, bf16[512,768]{1,0:T(8,128)(2,1)}, u32[]{:S(2)}) copy-start(bf16[512,768]{1,0:T(8,128)(2,1)} %gather_fusion) | copy-start | bytes 2359300
  67.5 12.5 %copy-start.7 = (bf16[1,512,768]{2,1,0:T(8,128)(2,1)S(1)}, bf16[1,512,768]{2,1,0:T(8,128)(2,1)}, u32[]{:S(2)}) copy-start(bf16[1,512,768]{2,1,0:T(8,128)(2,1)} %param.19) | copy-start | bytes 2359300
  67.5 12.5 %copy-start.31 = (bf16[768,768]{1,0:T(8,128)(2,1)S(1)}, bf16[768,768]{1,0:T(8,128)(2,1)}, u32[]{:S(2)}) copy-start(bf16[768,768]{1,0:T(8,128)(2,1)} %param.30) | copy-start | bytes 3538948
  67.5 12.5 %copy-start.33 = (f32[768]{0:T(1024)S(1)}, f32[768]{0:T(1024)}, u32[]{:S(2)}) copy-start(f32[768]{0:T(1024)} %param.31) | copy-start | bytes 9220
  80.0 1.2 copy-start.14
  80.0 1.5 copy-start.28
  80.0 1.5 copy-start.32
  80.0 1.5 copy-start.34
  80.0 22.2 %slice-start.2 = ((s8[4718592]{0:T(1024)(128)(4,1)}), s8[524288]{0:T(1024)(128)(4,1)S(1)}, s32[]{:S(2)}) async-start(s8[4718592]{0:T(1024)(128)(4,1)} %bitcast.156), calls=%async_computation.16 | async-start | bytes 1048576
  80.1 31.5 %slice-start = ((s8[4718592]{0:T(1024)(128)(4,1)}), s8[4194304]{0:T(1024)(128)(4,1)S(1)}, s32[]{:S(2)}) async-start(s8[4718592]{0:T(1024)(128)(4,1)} %bitcast.154), calls=%async_computation.14 | async-start | bytes 8388608
  81.1 36.0 %copy-start.10 = (f32[512,768]{1,0:T(8,128)}, f32[512,768]{1,0:T(8,128)S(1)}, u32[]{:S(2)}) copy-start(f32[512,768]{1,0:T(8,128)S(1)} %get-tuple-element.87) | copy-start | bytes 4718596
  81.5 35.6 %copy-start.27 = (f32[512]{0:T(512)}, f32[512]{0:T(512)S(1)}, u32[]{:S(2)}) copy-start(f32[512]{0:T(512)S(1)} %add_rsqrt_fusion) | copy-start | bytes 6148
  81.5 20.7 %copy-start.16 = (bf16[1,512,768]{2,1,0:T(8,128)(2,1)S(1)}, bf16[1,512,768]{2,1,0:T(8,128)(2,1)}, u32[]{:S(2)}) copy-start(bf16[1,512,768]{2,1,0:T(8,128)(2,1)} %param.22) | copy-start | bytes 2359300
  81.5 20.7 %slice-start.3 = ((s8[4718592]{0:T(1024)(128)(4,1)}), s8[4194304]{0:T(1024)(128)(4,1)S(1)}, s32[]{:S(2)}) async-start(s8[4718592]{0:T(1024)(128)(4,1)} %bitcast.156), calls=%async_computation.17 | async-start | bytes 8388608
  81.5 30.1 %slice-start.1 = ((s8[4718592]{0:T(1024)(128)(4,1)}), s8[524288]{0:T(1024)(128)(4,1)S(1)}, s32[]{:S(2)}) async-start(s8[4718592]{0:T(1024)(128)(4,1)} %bitcast.154), calls=%async_computation.15 | async-start | bytes 1048576
  118.5 1.2 copy-start.1
  126.3 3.0 copy-start.9
  126.3 3.0 copy-start.17
  156.7 7.2 copy-start.11
  166.0 125.9 %reduce-scatter.13.cloned.1.call-start = ((), (), s32[]{:S(2)}) async-start(), calls=%async_computation.8 | async-start | bytes 2433024 | tf_op jit(solution)/shard_map/reduce_scatter | solution.py:258
  169.9 221.6 %reduce-scatter.19.cloned.1.call-start = ((), (), s32[]{:S(2)}) async-start(), calls=%async_computation.13 | async-start | bytes 3244032
  181.1 5.7 copy-start.2
  181.1 5.7 copy-start.5
  181.1 5.7 copy-start.8
  181.1 5.7 copy-start.25
  181.1 5.7 copy-start.30
  199.4 333.1 %reduce-scatter.15.cloned.1.call-start = ((), (), s32[]{:S(2)}) async-start(), calls=%async_computation.9 | async-start | bytes 9732096 | tf_op jit(solution)/shard_map/reduce_scatter | solution.py:262
  208.6 466.0 %reduce-scatter.17.cloned.1.call-start = ((), (), s32[]{:S(2)}) async-start(), calls=%async_computation.10 | async-start | bytes 9732096 | tf_op jit(solution)/shard_map/reduce_scatter | solution.py:264
  217.1 0.7 copy-start.26
  217.2 581.9 %reduce-scatter.11.cloned.1.call-start = ((), (), s32[]{:S(2)}) async-start(), calls=%async_computation.7 | async-start | bytes 7299072 | tf_op jit(solution)/shard_map/reduce_scatter | solution.py:255
  225.5 7.4 copy-start.13
  225.5 7.4 copy-start.15
  225.5 8.4 %copy-start.21 = (f32[768]{0:T(1024)S(1)}, f32[768]{0:T(1024)}, u32[]{:S(2)}) copy-start(f32[768]{0:T(1024)} %get-tuple-element.69) | copy-start | bytes 9220
  225.5 8.4 %copy-start.22 = (f32[768]{0:T(1024)S(1)}, f32[768]{0:T(1024)}, u32[]{:S(2)}) copy-start(f32[768]{0:T(1024)} %get-tuple-element.77) | copy-start | bytes 9220
  225.5 8.4 %copy-start.23 = (f32[768]{0:T(1024)S(1)}, f32[768]{0:T(1024)}, u32[]{:S(2)}) copy-start(f32[768]{0:T(1024)} %get-tuple-element.71) | copy-start | bytes 9220
Sparse Core Ops, SparseCore 0:
  23.4 12.4 all-gather.4
  37.4 10.9 all-gather.6
  166.1 12.0 reduce-scatter.8
  184.8 100.2 reduce-scatter.12
  290.9 100.4 reduce-scatter.18
  397.8 134.6 reduce-scatter.14
  540.0 134.6 reduce-scatter.16
  680.9 118.1 reduce-scatter.10
where the time goes:
time: 811 us; the launch traced here: 806 us
  waiting for transfers between devices  514 us (63%)
  matrix products  155 us (19%)
  blocking collectives  42.6 us (5%)
  local copies, waits for them, and re-layouts  39.5 us (5%)
  other arithmetic  39.2 us (5%)
  between operations  14.8 us (2%)
    reduce_scatter x1, waiting for transfers between devices, body(): lax.psum_scatter(grad_w_down, ('dp', 'blk'), scatter_dimension=0, tiled=T...  142 us
    reduce_scatter x1, waiting for transfers between devices, body(): lax.psum_scatter(grad_w_up, ('dp', 'blk'), scatter_dimension=0, tiled=True)  141 us
    reduce_scatter x1, waiting for transfers between devices, body(): lax.psum_scatter(grad_w_qkv, ('dp', 'blk'), scatter_dimension=0, tiled=True)  124 us
    unnamed x9, waiting for transfers between devices  99.7 us
    unnamed x1, blocking collectives  42.6 us
    dot_general x4, matrix products, across(): lax.dot_general(left, right, (((0,), (0,)), ((), ())), preferred_element_...  28.9 us
    dot_general x4, matrix products, against(): lax.dot_general(left, weight, (((1,), (1,)), ((), ())), preferred_element...  22.3 us
    unnamed x91, local copies, waits for them, and re-layouts  20.8 us
  transfers between devices with their start and end apart: 8, of which 5 were waited for; matrix products, arithmetic and copies ran while one was open for 14% of the time, Pallas kernels for 0%

commit v1 on v0

v1 whole, which is shorter than its diff:
```python
import functools
import math

import jax
import jax.numpy as jnp
from jax import lax
from jax.experimental import pallas as pl
from jax.experimental.pallas import tpu as pltpu
from jax.sharding import PartitionSpec as P

HEADS = 12
HEAD_DIM = 64
PAIR = 2 * HEAD_DIM
EPSILON = 1e-06
SCORE_SCALE = 0.125
OWNERS = 32
EXTRA = 128
BF = jnp.bfloat16
F32 = jnp.float32
ALL = ("dp", "blk")
MIB = 1 << 20

NN = (((1,), (0,)), ((), ()))
NT = (((1,), (1,)), ((), ()))
TN = (((0,), (0,)), ((), ()))


def dot(left, right, dims=NN):
    return lax.dot_general(left, right, dims, preferred_element_type=F32)


def params(mib, *semantics):
    return pltpu.CompilerParams(
        vmem_limit_bytes=mib * MIB,
        dimension_semantics=semantics or None,
    )


def normalize(rows):
    centered = rows - jnp.mean(rows, -1, keepdims=True)
    inverse = lax.rsqrt(jnp.mean(centered * centered, -1, keepdims=True) + EPSILON)
    return centered * inverse, inverse


def norm_backward(grad, unit, inverse, gain):
    scaled = grad * gain
    return inverse * (
        scaled
        - jnp.mean(scaled, -1, keepdims=True)
        - unit * jnp.mean(scaled * unit, -1, keepdims=True)
    )


def lane_columns(row):
    return jnp.transpose(jnp.broadcast_to(row, (128, row.shape[1])), (1, 0))


def place_blocks(perm_ref, transposed, slots):
    size = transposed.shape[0] // OWNERS
    for owner in range(OWNERS):
        slots[perm_ref[owner]] = transposed[owner * size : (owner + 1) * size]


def embed_kernel(
    steps_kv, order_ref, mask_ref, tubes_ref, token_ref, table_ref, gain_ref, shift_ref,
    w_ref, bias_ref, scale_ref, emb_ref, hot_ref, q_ref, kv_ref, normed,
):
    step = pl.program_id(0)

    @pl.when(step == 0)
    def _():
        order = lane_columns(order_ref[...])
        mask = lane_columns(mask_ref[...])
        width = tubes_ref.shape[1]
        lanes = lax.broadcasted_iota(jnp.int32, order.shape, 1).astype(F32)
        for at in range(0, table_ref.shape[0], 128):
            hot_ref[:, at : at + 128] = jnp.where(order == lanes + at, 1.0, 0.0).astype(BF)
        positions = dot(hot_ref[...], table_ref[...])
        masks = jnp.concatenate([mask] * (width // 128), 1)
        rows = jnp.where(masks > 0.5, token_ref[...], tubes_ref[...].astype(F32)) + positions
        emb_ref[...] = rows
        unit, _ = normalize(rows)
        normed[...] = (unit * gain_ref[...] + shift_ref[...]).astype(BF)

    packed = dot(normed[...], w_ref[...]) + bias_ref[...]

    @pl.when(step < steps_kv)
    def _():
        kv_ref[...] = packed.astype(BF)

    @pl.when(step >= steps_kv)
    def _():
        q_ref[...] = (packed.astype(BF).astype(F32) * scale_ref[...]).astype(BF)


def embed(order, mask, tubes, token, table, gain, shift, w_qkv, bias):
    rows, width = tubes.shape
    length = table.shape[0]
    tile = width // 2
    steps_q = width // tile
    steps_kv = 2 * steps_q
    steps = steps_q + steps_kv
    whole = lambda shape: pl.BlockSpec(shape, lambda j: (0,) * len(shape))
    column = lambda j: (0, lax.rem(j + steps_q, steps))
    scale = jnp.full((1, tile), SCORE_SCALE, F32)
    return pl.pallas_call(
        functools.partial(embed_kernel, steps_kv),
        grid=(steps,),
        in_specs=[
            whole((1, rows)), whole((1, rows)), whole((rows, width)), whole((1, width)),
            whole((length, width)), whole((1, width)), whole((1, width)),
            pl.BlockSpec((width, tile), column), pl.BlockSpec((1, tile), column),
            whole((1, tile)),
        ],
        out_specs=[
            whole((rows, width)), whole((rows, length)),
            pl.BlockSpec((rows, tile), lambda j: (0, jnp.maximum(j - steps_kv, 0))),
            pl.BlockSpec((rows, tile), lambda j: (0, jnp.minimum(j, steps_kv - 1))),
        ],
        out_shape=[
            jax.ShapeDtypeStruct((rows, width), F32),
            jax.ShapeDtypeStruct((rows, length), BF),
            jax.ShapeDtypeStruct((rows, width), BF),
            jax.ShapeDtypeStruct((rows, 2 * width), BF),
        ],
        scratch_shapes=[pltpu.VMEM((rows, width), BF)],
        compiler_params=params(40, "arbitrary"),
        name="embed",
    )(order, mask, tubes, token, table, gain, shift, w_qkv, bias, scale)


def attend_kernel(blocks, tile, *refs):
    q_ref, key_refs, value_refs = refs[0], refs[1 : 1 + blocks], refs[1 + blocks : 1 + 2 * blocks]
    out_ref, log_ref = refs[1 + 2 * blocks :]
    keys = jnp.concatenate([ref[...] for ref in key_refs], 0)
    values = jnp.concatenate([ref[...] for ref in value_refs], 0)
    low_half = lax.broadcasted_iota(jnp.int32, (1, PAIR), 1) < HEAD_DIM
    one, zero = jnp.ones((), BF), jnp.zeros((), BF)
    value_halves = [jnp.where(low_half, values, one), jnp.where(low_half, one, values)]
    for at in range(0, q_ref.shape[0], tile):
        queries = q_ref[at : at + tile, :]
        tops, mixed = [], []
        for half in range(2):
            own = jnp.where(low_half, queries, zero) if half == 0 else jnp.where(low_half, zero, queries)
            scores = dot(own, keys, NT)
            top = jnp.max(scores, -1, keepdims=True)
            weights = jnp.exp(scores - top).astype(BF)
            tops.append(top)
            mixed.append(dot(weights, value_halves[half]))
        total = pltpu.roll(jnp.where(low_half, mixed[1], mixed[0]), HEAD_DIM, 1)
        out_ref[at : at + tile, :] = jnp.where(low_half, mixed[0], mixed[1]) / total
        logs = jnp.where(low_half, tops[0], tops[1]) + jnp.log(total)
        logs = jnp.transpose(logs, (1, 0))
        log_ref[0, 0, 0:1, at : at + tile] = logs[0:1]
        log_ref[0, 0, 1:2, at : at + tile] = logs[HEAD_DIM : HEAD_DIM + 1]


def attend(queries, held, clips):
    rows, width = queries.shape
    block = rows // clips
    pairs = width // PAIR
    blocks = len(held)
    spec = lambda off: pl.BlockSpec((block, PAIR), lambda c, p: (c, p + off))
    return pl.pallas_call(
        functools.partial(attend_kernel, blocks, min(block, 256)),
        grid=(clips, pairs),
        in_specs=[spec(0)] + [spec(0)] * blocks + [spec(pairs)] * blocks,
        out_specs=[spec(0), pl.BlockSpec((1, 1, 2, block), lambda c, p: (c, p, 0, 0))],
        out_shape=[
            jax.ShapeDtypeStruct((rows, width), F32),
            jax.ShapeDtypeStruct((clips, pairs, 2, block), F32),
        ],
        compiler_params=params(40, "arbitrary", "arbitrary"),
        name="attend",
    )(queries, *held, *held)


def attend_back_kernel(blocks, tile, *refs):
    q_ref, grad_ref, out_ref, log_ref = refs[:4]
    key_refs, value_refs = refs[4 : 4 + blocks], refs[4 + blocks : 4 + 2 * blocks]
    refs = refs[4 + 2 * blocks :]
    dq_ref, dkey_refs, dvalue_refs = refs[0], refs[1 : 1 + blocks], refs[1 + blocks :]
    low_half = lax.broadcasted_iota(jnp.int32, (1, PAIR), 1) < HEAD_DIM
    zero = jnp.zeros((), BF)
    queries, grads = q_ref[...], grad_ref[...]
    product = jnp.transpose(grads.astype(F32) * out_ref[...], (1, 0))
    dots = [
        jnp.sum(product[half * HEAD_DIM : (half + 1) * HEAD_DIM], 0, keepdims=True)
        for half in range(2)
    ]
    logs = [log_ref[0, 0, half : half + 1, :] for half in range(2)]
    dq = jnp.zeros(queries.shape, F32)
    for block in range(blocks):
        for at in range(0, key_refs[block].shape[0], tile):
            keys = key_refs[block][at : at + tile, :]
            values = value_refs[block][at : at + tile, :]
            dkeys, dvalues = [], []
            for half in range(2):
                pick = lambda x: jnp.where(low_half, x, zero) if half == 0 else jnp.where(low_half, zero, x)
                own_keys = pick(keys)
                scores = dot(own_keys, queries, NT)
                probs = jnp.exp(scores - logs[half])
                grad_probs = dot(pick(values), grads, NT)
                grad_scores = (probs * (grad_probs - dots[half])).astype(BF)
                dvalues.append(dot(probs.astype(BF), grads))
                dkeys.append(dot(grad_scores, queries))
                dq += dot(grad_scores, own_keys, TN)
            dkey_refs[block][at : at + tile, :] = jnp.where(low_half, *dkeys).astype(dkey_refs[block].dtype)
            dvalue_refs[block][at : at + tile, :] = jnp.where(low_half, *dvalues).astype(dvalue_refs[block].dtype)
    dq_ref[...] = (dq * SCORE_SCALE).astype(BF)


def attend_back(queries, grads, attended, logs, held, clips):
    rows, width = queries.shape
    block = rows // clips
    pairs = width // PAIR
    blocks = len(held)
    spec = lambda off: pl.BlockSpec((block, PAIR), lambda c, p: (c, p + off))
    kinds = [F32] + [BF] * (blocks - 1)
    outs = pl.pallas_call(
        functools.partial(attend_back_kernel, blocks, min(block, 256)),
        grid=(clips, pairs),
        in_specs=[spec(0)] * 3
        + [pl.BlockSpec((1, 1, 2, block), lambda c, p: (c, p, 0, 0))]
        + [spec(0)] * blocks
        + [spec(pairs)] * blocks,
        out_specs=[spec(0)] * (1 + 2 * blocks),
        out_shape=[jax.ShapeDtypeStruct((rows, width), kind) for kind in [BF] + kinds + kinds],
        compiler_params=params(40, "arbitrary", "arbitrary"),
        name="attend_back",
    )(queries, grads, attended, logs, *held, *held)
    return outs[0], outs[1 : 1 + blocks], outs[1 + blocks :]


def gelu_terms(x):
    bell = jnp.exp(x * x * -0.5)
    t = 1.0 / (1.0 + jnp.abs(x) * (0.3275911 * math.sqrt(0.5)))
    a1, a2, a3, a4, a5 = (0.5 * a for a in (0.254829592, -0.284496736, 1.421413741, -1.453152027, 1.061405429))
    tail = t * (a1 + t * (a2 + t * (a3 + t * (a4 + t * a5)))) * bell
    cdf = jnp.where(x >= 0.0, 1.0 - tail, tail)
    return x * cdf, cdf + x * bell * (1.0 / math.sqrt(2.0 * math.pi))


def middle_kernel(
    steps, perm_ref, att_ref, emb_ref, cot_ref, w_out_ref, bias_out_ref, gain_ref, shift_ref,
    w_up_ref, bias_up_ref, w_down_ref, bias_down_ref,
    output_ref, grad_after_ref, branch_ref, grad_att_ref, att_t_ref, normed_t_ref, act_t_ref, grad_pre_ref,
    bias_up_grad_ref, small_ref,
    normed, unit, inverse, result, grad_normed, slots,
):
    step = pl.program_id(0)
    rows, width = att_ref.shape

    def to_slots(array, out_ref):
        place_blocks(perm_ref, jnp.transpose(array, (1, 0)), slots)
        out_ref[...] = slots[...].reshape(width, rows).astype(BF)

    @pl.when(step == 0)
    def _():
        attended = att_ref[...]
        after = emb_ref[...] + dot(attended.astype(BF), w_out_ref[...]) + bias_out_ref[...]
        unit_rows, inverse_rows = normalize(after)
        normed_rows = unit_rows * gain_ref[...] + shift_ref[...]
        normed[...] = normed_rows.astype(BF)
        unit[...] = unit_rows
        inverse[...] = jnp.broadcast_to(inverse_rows, inverse.shape)
        result[...] = after + bias_down_ref[...]
        grad_normed[...] = jnp.zeros_like(grad_normed)
        to_slots(attended, att_t_ref)
        to_slots(normed_rows, normed_t_ref)

    pre_act = dot(normed[...], w_up_ref[...]) + bias_up_ref[...]
    active, slope = gelu_terms(pre_act)
    result[...] += dot(active.astype(BF), w_down_ref[...])
    grad_pre = (dot(cot_ref[...], w_down_ref[...], NT) * slope).astype(BF)
    grad_pre_ref[...] = grad_pre
    grad_normed[...] += dot(grad_pre, w_up_ref[...], NT)
    bias_up_grad_ref[...] = jnp.sum(grad_pre.astype(F32), 0, keepdims=True)
    active_t = jnp.transpose(active, (1, 0)).astype(BF)
    count = OWNERS // steps
    size = active_t.shape[0] // count
    for i in range(count):
        act_t_ref[perm_ref[step * count + i]] = active_t[i * size : (i + 1) * size]

    @pl.when(step == steps - 1)
    def _():
        output_ref[...] = result[...].astype(BF)
        cot = cot_ref[...].astype(F32)
        grad_rows = grad_normed[...]
        unit_rows = unit[...]
        grad_after = cot + norm_backward(grad_rows, unit_rows, inverse[:, 0:1], gain_ref[...])
        grad_after_ref[...] = grad_after
        branch = grad_after.astype(BF)
        branch_ref[...] = branch
        grad_att_ref[...] = dot(branch, w_out_ref[...], NT).astype(BF)
        total = lambda x: jnp.sum(x, 0, keepdims=True)
        small_ref[...] = jnp.concatenate(
            [
                total(grad_rows * unit_rows), total(grad_rows), total(branch.astype(F32)), total(cot),
                jnp.zeros((4, width), F32),
            ],
            0,
        )


def middle(perm, attended, embedded, cot, w_out, bias_out, gain, shift, w_up, bias_up, w_down, bias_down):
    rows, width = attended.shape
    hidden = w_up.shape[1]
    steps = 8
    tile = hidden // steps
    whole = lambda shape: pl.BlockSpec(shape, lambda j, s: (0,) * len(shape))
    across = lambda n: pl.BlockSpec((n, tile), lambda j, s: (0, j))
    return pl.pallas_call(
        functools.partial(middle_kernel, steps),
        grid_spec=pltpu.PrefetchScalarGridSpec(
            num_scalar_prefetch=1,
            grid=(steps,),
            in_specs=[
                whole((rows, width)), whole((rows, width)), whole((rows, width)), whole((width, width)),
                whole((1, width)), whole((1, width)), whole((1, width)),
                across(width), across(1), pl.BlockSpec((tile, width), lambda j, s: (j, 0)), whole((1, width)),
            ],
            out_specs=[
                whole((rows, width)), whole((rows, width)), whole((rows, width)), whole((rows, width)),
                whole((width, rows)), whole((width, rows)), whole((OWNERS, hidden // OWNERS, rows)), across(rows),
                across(1), whole((8, width)),
            ],
            scratch_shapes=[
                pltpu.VMEM((rows, width), BF), pltpu.VMEM((rows, width), F32), pltpu.VMEM((rows, 128), F32),
                pltpu.VMEM((rows, width), F32), pltpu.VMEM((rows, width), F32),
                pltpu.VMEM((OWNERS, width // OWNERS, rows), F32),
            ],
        ),
        out_shape=[
            jax.ShapeDtypeStruct((rows, width), BF),
            jax.ShapeDtypeStruct((rows, width), F32),
            jax.ShapeDtypeStruct((rows, width), BF),
            jax.ShapeDtypeStruct((rows, width), BF),
            jax.ShapeDtypeStruct((width, rows), BF),
            jax.ShapeDtypeStruct((width, rows), BF),
            jax.ShapeDtypeStruct((OWNERS, hidden // OWNERS, rows), BF),
            jax.ShapeDtypeStruct((rows, hidden), BF),
            jax.ShapeDtypeStruct((1, hidden), F32),
            jax.ShapeDtypeStruct((8, width), F32),
        ],
        compiler_params=params(56, "arbitrary"),
        name="middle",
    )(perm, attended, embedded, cot, w_out, bias_out, gain, shift, w_up, bias_up, w_down, bias_down)


def pack_kernel(parts, perm_ref, emb_ref, gain_ref, shift_ref, dq_ref, *refs):
    dkey_refs, dvalue_refs = refs[:parts], refs[parts : 2 * parts]
    packed_ref, normed_t_ref, sums_ref, slots = refs[2 * parts :]
    rows, width = emb_ref.shape
    add = lambda group: functools.reduce(jnp.add, [ref[...].astype(F32) for ref in group]).astype(BF)
    dq, dvalue = dq_ref[...], add(dvalue_refs)
    packed_ref[:, :width] = dq
    packed_ref[:, width : 2 * width] = add(dkey_refs)
    packed_ref[:, 2 * width :] = dvalue
    total = lambda x: jnp.sum(x.astype(F32), 0, keepdims=True)
    sums_ref[...] = jnp.concatenate([total(dq), total(dvalue), jnp.zeros((6, width), F32)], 0)
    unit, _ = normalize(emb_ref[...])
    place_blocks(perm_ref, jnp.transpose(unit * gain_ref[...] + shift_ref[...], (1, 0)), slots)
    normed_t_ref[...] = slots[...].reshape(width, rows).astype(BF)


def pack(perm, embedded, gain, shift, dq, dkeys, dvalues):
    rows, width = embedded.shape
    vmem = pl.BlockSpec(memory_space=pltpu.VMEM)
    return pl.pallas_call(
        functools.partial(pack_kernel, len(dkeys)),
        in_specs=[pl.BlockSpec(memory_space=pltpu.SMEM)] + [vmem] * (4 + 2 * len(dkeys)),
        out_specs=[vmem] * 3,
        out_shape=[
            jax.ShapeDtypeStruct((rows, 3 * width), BF),
            jax.ShapeDtypeStruct((width, rows), BF),
            jax.ShapeDtypeStruct((8, width), F32),
        ],
        scratch_shapes=[pltpu.VMEM((OWNERS, width // OWNERS, rows), F32)],
        compiler_params=params(48),
        name="pack",
    )(perm, embedded, gain, shift, dq, *dkeys, *dvalues)


def last_kernel(
    steps, perm_ref, packed_ref, w_ref, emb_ref, grad_after_ref, mask_ref, gain_ref, sums_ref, small_ref, bias_up_ref,
    tubes_ref, grad_t_ref, extra_ref, grad_normed, slots, extra_slots,
):
    step = pl.program_id(0)
    rows, width = emb_ref.shape
    term = dot(packed_ref[...], w_ref[...], NT)

    @pl.when(step == 0)
    def _():
        grad_normed[...] = term

    @pl.when(step > 0)
    def _():
        grad_normed[...] += term

    @pl.when(step == steps - 1)
    def _():
        unit, inverse = normalize(emb_ref[...])
        grad_rows = grad_normed[...]
        grad = grad_after_ref[...] + norm_backward(grad_rows, unit, inverse, gain_ref[...])
        mask = lane_columns(mask_ref[...])
        masks = jnp.concatenate([mask] * (width // 128), 1) > 0.5
        tubes_ref[...] = jnp.where(masks, 0.0, grad)
        total = lambda x: jnp.sum(x, 0, keepdims=True)
        place_blocks(perm_ref, jnp.transpose(grad, (1, 0)), slots)
        grad_t_ref[...] = slots[...].reshape(width, rows).astype(BF)
        stacked = jnp.concatenate(
            [
                total(jnp.where(masks, grad, 0.0)), total(grad_rows * unit), total(grad_rows), sums_ref[0:2, :],
                small_ref[0:4, :], bias_up_ref[...], jnp.zeros((EXTRA - 13, width), F32),
            ],
            0,
        )
        place_blocks(perm_ref, jnp.transpose(stacked, (1, 0)), extra_slots)
        extra_ref[...] = extra_slots[...].reshape(width, EXTRA).astype(BF)


def last(perm, packed, w_qkv, embedded, grad_after, mask, gain, sums, small, bias_up_rows):
    rows, width = embedded.shape
    steps = 6
    tile = packed.shape[1] // steps
    whole = lambda shape: pl.BlockSpec(shape, lambda j, s: (0,) * len(shape))
    across = lambda n: pl.BlockSpec((n, tile), lambda j, s: (0, j))
    return pl.pallas_call(
        functools.partial(last_kernel, steps),
        grid_spec=pltpu.PrefetchScalarGridSpec(
            num_scalar_prefetch=1,
            grid=(steps,),
            in_specs=[
                across(rows), across(width), whole((rows, width)), whole((rows, width)), whole((1, rows)),
                whole((1, width)), whole((8, width)), whole((8, width)), whole((4, width)),
            ],
            out_specs=[whole((rows, width)), whole((width, rows)), whole((width, EXTRA))],
            scratch_shapes=[
                pltpu.VMEM((rows, width), F32),
                pltpu.VMEM((OWNERS, width // OWNERS, rows), F32),
                pltpu.VMEM((OWNERS, width // OWNERS, EXTRA), F32),
            ],
        ),
        out_shape=[
            jax.ShapeDtypeStruct((rows, width), F32),
            jax.ShapeDtypeStruct((width, rows), BF),
            jax.ShapeDtypeStruct((width, EXTRA), BF),
        ],
        compiler_params=params(48, "arbitrary"),
        name="last",
    )(perm, packed, w_qkv, embedded, grad_after, mask, gain, sums, small, bias_up_rows)


def swap(array, bit):
    if bit == 0:
        return lax.ppermute(array, "blk", [(0, 1), (1, 0)])
    step = 1 << (bit - 1)
    return lax.ppermute(array, "dp", [(i, i ^ step) for i in range(OWNERS // 2)])


ROW_BITS = (1, 2, 3, 4)


def halve(array, left, bit):
    at = left.index(bit)
    rows, columns = array.shape
    after = rows >> (at + 1)
    cut = array.reshape(1 << at, 2, after, columns)
    keep, send = cut[:, 0].reshape(rows // 2, columns), cut[:, 1].reshape(rows // 2, columns)
    received = swap(send, bit)
    total = keep.astype(F32) + received.astype(F32)
    return total, tuple(b for b in left if b != bit)


def reduce_chain(array, order):
    left = ROW_BITS
    for bit in order:
        array, left = halve(array.astype(BF), left, bit)
    return array


ORDERS = ((1, 2, 3, 4), (2, 1, 3, 4), (3, 1, 2, 4))


def weight_grad(left, right):
    rows = left.shape[0] // 2
    other = dot(left[rows:], right).astype(BF)
    received = swap(other, 0)
    return (dot(left[:rows], right) + received.astype(F32)).astype(BF)


def scatter_sum(array, parts):
    width = array.shape[1] // parts
    cuts = [array[:, i * width : (i + 1) * width] for i in range(parts)]
    return jnp.concatenate([reduce_chain(cut, ORDERS[i % 3]) for i, cut in enumerate(cuts)], 1)


def body(
    paired,
    tubes, tube_mask, tube_order, cotangent, mask_token, pos_table, ln1_gain, ln1_bias, w_qkv, bias_q, bias_v,
    w_out, bias_out, ln2_gain, ln2_bias, w_up, bias_up, w_down, bias_down,
):
    clips, block, width = tubes.shape
    rows = clips * block
    blocks = lax.axis_size("blk")
    devices = blocks * lax.axis_size("dp")
    row = lambda x: x.reshape(1, -1)
    owners = jnp.arange(OWNERS, dtype=jnp.int32)
    if paired:
        me = lax.axis_index("dp") * 2 + lax.axis_index("blk")
        apart = jnp.bitwise_xor(owners, me)
        perm = sum(((apart >> bit) & 1) << (4 - bit) for bit in range(5))
    else:
        perm = owners

    order = tube_order.reshape(1, rows).astype(F32)
    mask = tube_mask.reshape(1, rows).astype(F32)
    cot = cotangent.reshape(rows, width)
    bias = jnp.concatenate([bias_q, jnp.zeros_like(bias_q), bias_v]).reshape(1, -1)
    embedded, hot, queries, kv = embed(
        order, mask, tubes.reshape(rows, width), row(mask_token), pos_table, row(ln1_gain), row(ln1_bias), w_qkv, bias
    )
    held = [kv] + [
        lax.ppermute(kv, "blk", [(i, (i + s) % blocks) for i in range(blocks)]) for s in range(1, blocks)
    ]
    attended, logs = attend(queries, held, clips)
    (
        output, grad_after, branch, grad_att, att_t, normed_t, act_t, grad_pre, bias_up_grad, small,
    ) = middle(
        perm, attended, embedded, cot, w_out, row(bias_out), row(ln2_gain), row(ln2_bias), w_up, row(bias_up),
        w_down, row(bias_down),
    )
    act_t = act_t.reshape(-1, rows)
    if paired:
        total_down = weight_grad(act_t, cot)
        total_up = weight_grad(normed_t, grad_pre)
        total_out = weight_grad(att_t, branch)
        grad_w_down = scatter_sum(total_down, 3)
        grad_w_up = scatter_sum(total_up, 3)
        grad_w_out = scatter_sum(total_out, 1)
    else:
        spread = lambda left, right: lax.psum_scatter(dot(left, right), ALL, scatter_dimension=0, tiled=True)
        grad_w_down = spread(act_t, cot)
        grad_w_up = spread(normed_t, grad_pre)
        grad_w_out = spread(att_t, branch)

    dq, dkeys, dvalues = attend_back(queries, grad_att, attended, logs, held, clips)
    home = lambda x, s: lax.ppermute(x, "blk", [((i + s) % blocks, i) for i in range(blocks)])
    dkeys = [dkeys[0]] + [home(dkeys[s], s) for s in range(1, blocks)]
    dvalues = [dvalues[0]] + [home(dvalues[s], s) for s in range(1, blocks)]
    packed, normed_one_t, sums = pack(perm, embedded, row(ln1_gain), row(ln1_bias), dq, dkeys, dvalues)
    bias_up_rows = bias_up_grad.reshape(devices, -1, width // devices).swapaxes(0, 1).reshape(-1, width)
    grad_tubes, grad_t, extra = last(
        perm, packed, w_qkv, embedded, grad_after, mask, row(ln1_gain), sums, small, bias_up_rows
    )
    if paired:
        grad_w_qkv = scatter_sum(weight_grad(normed_one_t, packed), 3)
        total_pos = weight_grad(grad_t, hot)
        half = extra.shape[0] // 2
        total_extra = (extra[:half].astype(F32) + swap(extra[half:], 0).astype(F32)).astype(BF)
        tail = scatter_sum(jnp.concatenate([total_pos, total_extra], 1), 3)
        grad_pos, extra = tail[:, : hot.shape[1]], tail[:, hot.shape[1] :]
    else:
        grad_w_qkv = spread(normed_one_t, packed)
        grad_pos = spread(grad_t, hot)
        extra = lax.psum_scatter(extra.astype(F32), ALL, scatter_dimension=0, tiled=True)
    vector = [extra[:, i] for i in range(9)]
    grad_bias_up = extra[:, 9:13].T.reshape(-1)
    mask_grad, gain_one, shift_one, grad_bias_q, grad_bias_v, gain_two, shift_two, grad_bias_out, grad_bias_down = vector
    return (
        output.reshape(clips, block, width),
        grad_tubes.reshape(clips, block, width),
        mask_grad,
        grad_pos.T,
        gain_one,
        shift_one,
        grad_w_qkv,
        grad_bias_q,
        grad_bias_v,
        grad_w_out,
        grad_bias_out,
        gain_two,
        shift_two,
        grad_w_up,
        grad_bias_up,
        grad_w_down,
        grad_bias_down,
    )


def solution(mesh):
    split = P("dp", "blk", None)
    flat = P("dp", "blk")
    in_specs = (split, flat, flat, split) + (P(),) * 15
    one, two = P(ALL), P(ALL, None)
    out_specs = (split, split, one, P(None, ALL), one, one, two, one, one, two, one, one, one, two, one, two, one)
    paired = mesh.shape["blk"] == 2 and mesh.shape["dp"] == OWNERS // 2
    return jax.shard_map(
        functools.partial(body, paired), mesh=mesh, in_specs=in_specs, out_specs=out_specs, check_vma=False
    )
```

time: 811 us -> 255 us (0.31)
  waiting for transfers between devices: 514 us -> 37.9 us
  matrix products: 155 us -> 21.8 us
  Pallas kernels: 0 us -> 86.6 us
  starting transfers between devices: 0.89 us -> 70 us
  blocking collectives: 42.6 us -> 0 us
  other arithmetic: 39.2 us -> 9.11 us
  local copies, waits for them, and re-layouts: 39.5 us -> 25.1 us
  between operations: 14.8 us -> 1.84 us
    reduce_scatter x5 -> x0, waiting for transfers between devices: 408 us -> none  [the longest x1 142 us: body(): lax.psum_scatter(grad_w_down, ('dp', 'blk'), scatter_dimension=0, tiled=T...]
    dot_general x18 -> x10, matrix products: 155 us -> 21.8 us  [dot(): return lax.dot_general(left, right, dims, preferred_element_type=F32)]
    unnamed x9 -> x0, waiting for transfers between devices: 99.7 us -> none
    pallas_call x0 -> x6, Pallas kernels: none -> 86.6 us  [the longest x1 30.9 us: middle(): pl.pallas_call(functools.partial(middle_kernel, steps), grid_spec=pltpu.P...]
    ppermute x0 -> x61, starting transfers between devices: none -> 70 us  [the longest x52 67.7 us: swap(): lax.ppermute(array, 'dp', [(i, i ^ step) for i in range(OWNERS // 2)])]
    unnamed x1 -> x0, blocking collectives: 42.6 us -> none
    ppermute x0 -> x61, waiting for transfers between devices: none -> 37.9 us  [the longest x52 37.7 us: swap(): lax.ppermute(array, 'dp', [(i, i ^ step) for i in range(OWNERS // 2)])]
    reduce_sum x8 -> x0, other arithmetic: 22.3 us -> none  [the longest x1 11 us: body(): run_total = jnp.sum(weights, -1)]
  transfers between devices with their start and end apart: 8 -> 61, of which waited for: 5 -> 21; matrix products, arithmetic and copies ran while one was open for 14% -> 15% of each run, Pallas kernels for 0% -> 14%
where the time goes in v1:
time: 255 us; the launch traced here: 252 us
  Pallas kernels  86.6 us (34%)
  starting transfers between devices  70 us (27%)
  waiting for transfers between devices  37.9 us (15%)
  local copies, waits for them, and re-layouts  25.1 us (10%)
  matrix products  21.8 us (9%)
  other arithmetic  9.11 us (4%)
    ppermute x52, starting transfers between devices, swap(): lax.ppermute(array, 'dp', [(i, i ^ step) for i in range(OWNERS // 2)])  67.7 us
    ppermute x52, waiting for transfers between devices, swap(): lax.ppermute(array, 'dp', [(i, i ^ step) for i in range(OWNERS // 2)])  37.7 us
    pallas_call x1, Pallas kernels, middle(): pl.pallas_call(functools.partial(middle_kernel, steps), grid_spec=pltpu.P...  30.9 us
    dot_general x10, matrix products, dot(): return lax.dot_general(left, right, dims, preferred_element_type=F32)  21.8 us
    pallas_call x1, Pallas kernels, attend_back(): pl.pallas_call(functools.partial(attend_back_kernel, blocks, min(block, 2...  20.8 us
    pallas_call x1, Pallas kernels, attend(): pl.pallas_call(functools.partial(attend_kernel, blocks, min(block, 256)),...  13.7 us
    unnamed x78, local copies, waits for them, and re-layouts  11.2 us
    pallas_call x1, Pallas kernels, last(): pl.pallas_call(functools.partial(last_kernel, steps), grid_spec=pltpu.Pre...  9.94 us
  transfers between devices with their start and end apart: 61, of which 21 were waited for; matrix products, arithmetic and copies ran while one was open for 15% of the time, Pallas kernels for 14%

profile of v1, /device:TPU:0, one launch (start us, length us, event | category | flops | bytes accessed | tf_op | source)
XLA Modules:
  0.0 252.3 jit_solution(5578026000686215727)
XLA Ops:
  4.8 2.0 copy-done
  6.8 1.4 copy-done.9
  8.2 1.1 copy-done.14
  9.4 6.3 %embed.1 = (f32[512,768]{1,0:T(8,128)S(1)}, bf16[512,1024]{1,0:T(8,128)(2,1)S(1)}, bf16[512,768]{1,0:T(8,128)(2,1)S(1)}, bf16[512,1536]{1,0:T(8,128)(2,1)S(1)}) custom-call(f32[1,512]{1,0:T(1,128)S(1)} %convert_element_type.645.order_ref, f32[1,512]{1,0:T(1,128)S(1)} %convert_element_type.646.mask_ref, bf16[512,768]{1,0:T(8,128)(2,1)S(1)} %bitcast.420, ...), custom_call_target="tpu_custom_call" | custom-call | tf_op jit(solution)/shard_map/embed/pallas_call | solution.py:106
  15.7 1.2 copy-done.1
  22.3 1.1 copy-done.6
  23.4 13.7 %attend.1 = (f32[512,768]{1,0:T(8,128)S(1)}, f32[1,6,2,512]{3,2,1,0:T(2,128)S(1)}) custom-call(bf16[512,768]{1,0:T(8,128)(2,1)S(1)} %copy-done.6, bf16[512,1536]{1,0:T(8,128)(2,1)S(1)} %get-tuple-element.45.refs_1_.refs_3_.refs_4_.refs_6_, bf16[512,1536]{1,0:T(8,128)(2,1)S(1)} %collective-permute-done.refs_2_.refs_4_.refs_5_.refs_7_, ...), custom_call_target="tpu_custom_call" | custom-call | tf_op jit(solution)/shard_map/attend/pallas_call | solution.py:164
  37.2 1.1 copy-done.3
  38.3 30.9 %middle.1 = (bf16[512,768]{1,0:T(8,128)(2,1)}, f32[512,768]{1,0:T(8,128)}, bf16[512,768]{1,0:T(8,128)(2,1)}, bf16[512,768]{1,0:T(8,128)(2,1)}, bf16[768,512]{1,0...) custom-call(s32[32]{0:T(128)} %shift-left_add_fusion.perm_ref, ...), custom_call_target="tpu_custom_call" | custom-call | tf_op jit(solution)/shard_map/middle/pallas_call | solution.py:313
  69.2 1.7 convolution_convert_fusion.4
  71.4 3.5 %fusion.58 = (bf16[16,96,512]{2,1,0:T(8,128)(2,1)}, bf16[16,96,512]{2,1,0:T(8,128)(2,1)S(1)}) fusion(bf16[32,96,512]{2,1,0:T(8,128)(2,1)} %get-tuple-element.70), kind=kLoop, calls=%fused_computation.223 | loop fusion | bytes 6291456 | tf_op jit(solution)/shard_map/slice | solution.py:490
  74.9 2.8 %convolution_convert_fusion.2 = bf16[1536,768]{1,0:T(8,128)(2,1)} fusion(bf16[1536,512]{1,0:T(8,128)(2,1)S(1)} %bitcast.434, bf16[1,512,768]{2,1,0:T(8,128)(2,1)S(1)} %copy-done.24), kind=kOutput, calls=%fused_computation.6 | convolution fusion | flops 1209139200 | bytes 4718592 | tf_op jit(solution)/shard_map/dot_general | solution.py:29
  77.9 20.8 %attend_back.1 = (bf16[512,768]{1,0:T(8,128)(2,1)S(1)}, f32[512,768]{1,0:T(8,128)S(1)}, bf16[512,768]{1,0:T(8,128)(2,1)}, f32[512,768]{1,0:T(8,128)S(1)}, bf16[512,768]{1,0:T(8,128)(2,1)}) custom-call(bf16[512,768]{1,0:T(8,128)(2,1)S(1)} %copy-done.7, bf16[512,768]{1,0:T(8,128)(2,1)S(1)} %copy-done.17, f32[512,768]{1,0:T(8,128)S(1)} %copy-done.4, ...), custom_call_target="tpu_custom_call" | custom-call | tf_op jit(solution)/shard_map/attend_back/pallas_call | solution.py:220
  100.7 2.9 %collective-permute-start.31 = (bf16[192,768]{1,0:T(8,128)(2,1)}, bf16[192,768]{1,0:T(8,128)(2,1)S(1)}, u32[]{:S(2)}, u32[]{:S(2)}) collective-permute-start(bf16[192,768]{1,0:T(8,128)(2,1)} %slice_bitcast_fusion.4), channel_id=1, source_target_pairs={{0,2},{2,0},{4,6},{6,4},{8,10},{10,8},{12,14},{14,12},{16,18},{18,... | collective-permute-start | bytes 884744 | tf_op jit(solution)/shard_map/ppermute | solution.py:459
  103.7 2.8 %convolution_convert_fusion = bf16[384,3072]{1,0:T(8,128)(2,1)} fusion(bf16[512,3072]{1,0:T(8,128)(2,1)S(1)} %copy-done.33, bf16[768,512]{1,0:T(8,128)(2,1)S(1)} %copy-done.35), kind=kOutput, calls=%fused_computation.4 | convolution fusion | flops 1209139200 | bytes 5898240 | tf_op jit(solution)/shard_map/dot_general | solution.py:29
  109.5 1.1 copy-done.16
  110.6 4.9 %pack.1 = (bf16[512,2304]{1,0:T(8,128)(2,1)}, bf16[768,512]{1,0:T(8,128)(2,1)S(1)}, f32[8,768]{1,0:T(8,128)S(1)}) custom-call(s32[32]{0:T(128)S(1)} %copy-done.19, f32[512,768]{1,0:T(8,128)S(1)} %copy-done.2, f32[1,768]{1,0:T(1,128)S(1)} %reshape.350.gain_ref, f32[1,768]{1,0:T(1,128)S(1)} %reshape.351.shift_ref, bf16[512,768]{1,0:T(8,128)(2,1)S(1)} %copy-done.16, ...), custom_call_target="tpu_custom_call" | custom-call | tf_op jit(solution)/shard_map/pack/pallas_call | solution.py:370
  115.7 1.6 collective-permute-start.32
  117.2 4.1 %convolution_convert_fusion.1 = bf16[384,2304]{1,0:T(8,128)(2,1)} fusion(bf16[512,2304]{1,0:T(8,128)(2,1)} %get-tuple-element.56.packed_ref, bf16[768,512]{1,0:T(8,128)(2,1)S(1)} %get-tuple-element.65), kind=kOutput, calls=%fused_computation.5 | convolution fusion | flops 906854400 | bytes 4521984 | tf_op jit(solution)/shard_map/dot_general | solution.py:29
  121.6 9.9 %last.1 = (f32[512,768]{1,0:T(8,128)}, bf16[768,512]{1,0:T(8,128)(2,1)S(1)}, bf16[768,128]{1,0:T(8,128)(2,1)S(1)}) custom-call(s32[32]{0:T(128)S(1)} %copy-done.19, bf16[512,2304]{1,0:T(8,128)(2,1)} %get-tuple-element.56.packed_ref, bf16[768,2304]{1,0:T(8,128)(2,1)} %w_ref.3, f32[512,768]{1,0:T(8,128)S(1)} %copy-done.2, f32[512,768]{1,0:T(8,128)S(1)} %copy-done.8, ...), custom_call_target="tpu_custom_call" | custom-call | tf_op jit(solution)/shard_map/last/pallas_call | solution.py:429
  131.9 1.7 collective-permute-start.33
  134.2 2.2 collective-permute-done.33
  136.4 2.7 %collective-permute-start.34 = (bf16[24,768]{1,0:T(8,128)(2,1)S(1)}, bf16[24,768]{1,0:T(8,128)(2,1)S(1)}, u32[]{:S(2)}, u32[]{:S(2)}) collective-permute-start(bf16[24,768]{1,0:T(8,128)(2,1)S(1)} %slice_bitcast_fusion.68), channel_id=1, source_target_pairs={{0,16},{2,18},{4,20},{6,22},{8,24},{10,26},{12,28},{14,30},{16,0},... | collective-permute-start | bytes 110600 | tf_op jit(solution)/shard_map/ppermute | solution.py:459
  139.1 2.2 collective-permute-done.34
  143.8 4.1 %collective-permute-done.9 = bf16[192,384]{1,0:T(8,128)(2,1)S(1)} collective-permute-done((bf16[192,384]{1,0:T(8,128)(2,1)S(1)}, bf16[192,384]{1,0:T(8,128)(2,1)S(1)}, u32[]{:S(2)}, u32[]{:S(2)}) %collective-permute-start.9) | collective-permute-done | bytes 147488 | tf_op jit(solution)/shard_map/ppermute | solution.py:459
  147.9 1.9 collective-permute-start.5
  150.5 2.5 %collective-permute-done.5 = bf16[192,384]{1,0:T(8,128)(2,1)S(1)} collective-permute-done((bf16[192,384]{1,0:T(8,128)(2,1)S(1)}, bf16[192,384]{1,0:T(8,128)(2,1)S(1)}, u32[]{:S(2)}, u32[]{:S(2)}) %collective-permute-start.5) | collective-permute-done | bytes 147488 | tf_op jit(solution)/shard_map/ppermute | solution.py:459
  155.3 2.1 collective-permute-done.14
  157.4 1.9 collective-permute-start.11
  160.2 1.2 collective-permute-done.11
  161.9 1.7 collective-permute-done.15
  163.6 3.3 %collective-permute-start.12 = (bf16[24,384]{1,0:T(8,128)(2,1)S(1)}, bf16[24,384]{1,0:T(8,128)(2,1)S(1)}, u32[]{:S(2)}, u32[]{:S(2)}) collective-permute-start(bf16[24,384]{1,0:T(8,128)(2,1)S(1)} %slice_bitcast_fusion.84), channel_id=1, source_target_pairs={{0,16},{2,18},{4,20},{6,22},{8,24},{10,26},{12,28},{14,30},{16,0},... | collective-permute-start | bytes 55304 | tf_op jit(solution)/shard_map/ppermute | solution.py:459
  167.0 2.1 collective-permute-start.16
  169.1 2.5 collective-permute-start.8
  171.6 2.2 collective-permute-done.8
  176.1 3.0 %add_convert_fusion = bf16[1536,768]{1,0:T(8,128)(2,1)S(1)} fusion(bf16[1536,768]{1,0:T(8,128)(2,1)} %collective-permute-done.48, bf16[1536,512]{1,0:T(8,128)(2,1)S(1)} %bitcast.433, bf16[1,512,768]{2,1,0:T(8,128)(2,1)S(1)} %copy-done.25), kind=kOutput, calls=%fused_computation | convolution fusion | flops 1211498496 | bytes 7077888 | tf_op jit(solution)/shard_map/dot_general | solution.py:29
  180.4 2.0 collective-permute-start.57
  182.4 3.1 %add_convert_fusion.1 = bf16[384,3072]{1,0:T(8,128)(2,1)S(1)} fusion(bf16[384,3072]{1,0:T(8,128)(2,1)} %collective-permute-done.35, bf16[512,3072]{1,0:T(8,128)(2,1)S(1)} %copy-done.34, bf16[768,512]{1,0:T(8,128)(2,1)S(1)} %copy-done.36), kind=kOutput, calls=%fused_computation.1 | convolution fusion | flops 1211498496 | bytes 8257536 | tf_op jit(solution)/shard_map/dot_general | solution.py:29
  185.8 1.5 collective-permute-start.36
  187.5 1.6 collective-permute-start.40
  189.1 2.6 %fusion = bf16[384,2304]{1,0:T(8,128)(2,1)S(1)} fusion(bf16[512,2304]{1,0:T(8,128)(2,1)S(1)} %copy-done.22, bf16[384,2304]{1,0:T(8,128)(2,1)} %collective-permute-done.17, bf16[768,512]{1,0:T(8,128)(2,1)S(1)} %copy-done.21), kind=kOutput, calls=%fused_computation.3 | convolution fusion | flops 908623872 | bytes 6291456 | tf_op jit(solution)/shard_map/dot_general | solution.py:29
  192.0 1.2 collective-permute-start.44
  194.1 4.5 %collective-permute-done.36 = bf16[192,1024]{1,0:T(8,128)(2,1)S(1)} collective-permute-done((bf16[192,1024]{1,0:T(8,128)(2,1)S(1)}, bf16[192,1024]{1,0:T(8,128)(2,1)S(1)}, u32[]{:S(2)}, u32[]{:S(2)}) %collective-permute-start.36) | collective-permute-done | bytes 393248 | tf_op jit(solution)/shard_map/ppermute | solution.py:459
  198.6 1.4 collective-permute-start.22
  200.5 1.7 collective-permute-start.50
  203.1 1.9 collective-permute-done.18
  204.9 1.5 collective-permute-start.58
  207.5 1.5 collective-permute-start.37
  209.2 1.2 collective-permute-start.41
  212.5 2.0 collective-permute-done.58
  215.0 1.7 collective-permute-start.27
  216.7 1.3 collective-permute-done.41
  218.0 1.5 collective-permute-start.51
  220.1 1.5 collective-permute-start.55
  222.3 1.6 collective-permute-start.38
  224.8 1.4 collective-permute-start.46
  227.1 1.4 collective-permute-start.24
  229.7 2.5 collective-permute-start.52
  232.8 2.5 collective-permute-start.60
  236.0 2.5 collective-permute-start.43
  238.5 2.4 collective-permute-done.39
  240.9 2.0 collective-permute-done.43
  243.9 2.0 collective-permute-done.47
  246.7 2.8 %collective-permute-start.29 = (bf16[24,768]{1,0:T(8,128)(2,1)S(1)}, bf16[24,768]{1,0:T(8,128)(2,1)S(1)}, u32[]{:S(2)}, u32[]{:S(2)}) collective-permute-start(bf16[24,768]{1,0:T(8,128)(2,1)S(1)} %slice_bitcast_fusion.70), channel_id=1, source_target_pairs={{0,16},{2,18},{4,20},{6,22},{8,24},{10,26},{12,28},{14,30},{16,0},... | collective-permute-start | bytes 110600 | tf_op jit(solution)/shard_map/ppermute | solution.py:459
  (290 shorter events, 43.2 us)
Async XLA Ops:
  18.8 3.5 %collective-permute-start = (bf16[512,1536]{1,0:T(8,128)(2,1)S(1)}, bf16[512,1536]{1,0:T(8,128)(2,1)S(1)}, u32[]{:S(2)}, u32[]{:S(2)}) collective-permute-start(bf16[512,1536]{1,0:T(8,128)(2,1)S(1)} %get-tuple-element.45.refs_1_.refs_3_.refs_4_.refs_6_), channel_id=1, source_target_pairs={{0,1},{1,0},{2,3},{3,2},{4,5},{5,4},{6,7},{7,6},{8,9},{9,8},{10,11... | collective-permute-start | bytes 4718600 | tf_op jit(solution)/shard_map/ppermute | solution.py:525
  70.9 28.3 %collective-permute-start.30 = (bf16[384,768]{1,0:T(8,128)(2,1)S(1)}, bf16[384,768]{1,0:T(8,128)(2,1)S(1)}, u32[]{:S(2)}, u32[]{:S(2)}) collective-permute-start(bf16[384,768]{1,0:T(8,128)(2,1)S(1)} %convolution_convert_fusion.4), channel_id=1, source_target_pairs={{0,1},{1,0},{2,3},{3,2},{4,5},{5,4},{6,7},{7,6},{8,9},{9,8},{10,11... | collective-permute-start | bytes 1769480 | tf_op jit(solution)/shard_map/ppermute | solution.py:457
  77.7 98.4 %collective-permute-start.48 = (bf16[1536,768]{1,0:T(8,128)(2,1)}, bf16[1536,768]{1,0:T(8,128)(2,1)}, u32[]{:S(2)}, u32[]{:S(2)}) collective-permute-start(bf16[1536,768]{1,0:T(8,128)(2,1)} %convolution_convert_fusion.2), channel_id=1, source_target_pairs={{0,1},{1,0},{2,3},{3,2},{4,5},{5,4},{6,7},{7,6},{8,9},{9,8},{10,11... | collective-permute-start | bytes 7077896 | tf_op jit(solution)/shard_map/ppermute | solution.py:457
  77.8 25.8 %copy-start.33 = (bf16[512,3072]{1,0:T(8,128)(2,1)S(1)}, bf16[512,3072]{1,0:T(8,128)(2,1)}, u32[]{:S(2)}) copy-start(bf16[512,3072]{1,0:T(8,128)(2,1)} %get-tuple-element.69) | copy-start | bytes 9437188
  98.6 10.8 %collective-permute-start.1 = (bf16[512,768]{1,0:T(8,128)(2,1)}, bf16[512,768]{1,0:T(8,128)(2,1)S(1)}, u32[]{:S(2)}, u32[]{:S(2)}) collective-permute-start(bf16[512,768]{1,0:T(8,128)(2,1)} %get-tuple-element.53), channel_id=1, source_target_pairs={{1,0},{0,1},{3,2},{2,3},{5,4},{4,5},{7,6},{6,7},{9,8},{8,9},{11,10... | collective-permute-start | bytes 2359304 | tf_op jit(solution)/shard_map/ppermute | solution.py:549
  99.1 10.3 %collective-permute-start.2 = (bf16[512,768]{1,0:T(8,128)(2,1)}, bf16[512,768]{1,0:T(8,128)(2,1)S(1)}, u32[]{:S(2)}, u32[]{:S(2)}) collective-permute-start(bf16[512,768]{1,0:T(8,128)(2,1)} %get-tuple-element.55), channel_id=1, source_target_pairs={{1,0},{0,1},{3,2},{2,3},{5,4},{4,5},{7,6},{6,7},{9,8},{8,9},{11,10... | collective-permute-start | bytes 2359304 | tf_op jit(solution)/shard_map/ppermute | solution.py:549
  100.7 14.8 %collective-permute-start.31 = (bf16[192,768]{1,0:T(8,128)(2,1)}, bf16[192,768]{1,0:T(8,128)(2,1)S(1)}, u32[]{:S(2)}, u32[]{:S(2)}) collective-permute-start(bf16[192,768]{1,0:T(8,128)(2,1)} %slice_bitcast_fusion.4), channel_id=1, source_target_pairs={{0,2},{2,0},{4,6},{6,4},{8,10},{10,8},{12,14},{14,12},{16,18},{18,... | collective-permute-start | bytes 884744 | tf_op jit(solution)/shard_map/ppermute | solution.py:459
  106.5 76.0 %collective-permute-start.35 = (bf16[384,3072]{1,0:T(8,128)(2,1)}, bf16[384,3072]{1,0:T(8,128)(2,1)}, u32[]{:S(2)}, u32[]{:S(2)}) collective-permute-start(bf16[384,3072]{1,0:T(8,128)(2,1)} %convolution_convert_fusion), channel_id=1, source_target_pairs={{0,1},{1,0},{2,3},{3,2},{4,5},{5,4},{6,7},{7,6},{8,9},{9,8},{10,11... | collective-permute-start | bytes 7077896 | tf_op jit(solution)/shard_map/ppermute | solution.py:457
  115.7 16.2 %collective-permute-start.32 = (bf16[96,768]{1,0:T(8,128)(2,1)S(1)}, bf16[96,768]{1,0:T(8,128)(2,1)S(1)}, u32[]{:S(2)}, u32[]{:S(2)}) collective-permute-start(bf16[96,768]{1,0:T(8,128)(2,1)S(1)} %slice_bitcast_fusion.20), channel_id=1, source_target_pairs={{0,4},{2,6},{4,0},{6,2},{8,12},{10,14},{12,8},{14,10},{16,20},{18,... | collective-permute-start | bytes 442376 | tf_op jit(solution)/shard_map/ppermute | solution.py:459
  121.3 66.2 %collective-permute-start.17 = (bf16[384,2304]{1,0:T(8,128)(2,1)}, bf16[384,2304]{1,0:T(8,128)(2,1)}, u32[]{:S(2)}, u32[]{:S(2)}) collective-permute-start(bf16[384,2304]{1,0:T(8,128)(2,1)} %convolution_convert_fusion.1), channel_id=1, source_target_pairs={{0,1},{1,0},{2,3},{3,2},{4,5},{5,4},{6,7},{7,6},{8,9},{9,8},{10,11... | collective-permute-start | bytes 5308424 | tf_op jit(solution)/shard_map/ppermute | solution.py:457
  131.5 4.9 %collective-permute-start.4 = (bf16[384,128]{1,0:T(8,128)(2,1)S(1)}, bf16[384,128]{1,0:T(8,128)(2,1)S(1)}, u32[]{:S(2)}, u32[]{:S(2)}) collective-permute-start(bf16[384,128]{1,0:T(8,128)(2,1)S(1)} %slice.437), channel_id=1, source_target_pairs={{0,1},{1,0},{2,3},{3,2},{4,5},{5,4},{6,7},{7,6},{8,9},{9,8},{10,11... | collective-permute-start | bytes 294920 | tf_op jit(solution)/shard_map/ppermute | solution.py:457
  131.9 4.4 %collective-permute-start.33 = (bf16[48,768]{1,0:T(8,128)(2,1)S(1)}, bf16[48,768]{1,0:T(8,128)(2,1)S(1)}, u32[]{:S(2)}, u32[]{:S(2)}) collective-permute-start(bf16[48,768]{1,0:T(8,128)(2,1)S(1)} %slice_bitcast_fusion.42), channel_id=1, source_target_pairs={{0,8},{2,10},{4,12},{6,14},{8,0},{10,2},{12,4},{14,6},{16,24},{18,... | collective-permute-start | bytes 221192 | tf_op jit(solution)/shard_map/ppermute | solution.py:459
  136.4 5.6 %collective-permute-start.3 = (bf16[384,1024]{1,0:T(8,128)(2,1)S(1)}, bf16[384,1024]{1,0:T(8,128)(2,1)S(1)}, u32[]{:S(2)}, u32[]{:S(2)}) collective-permute-start(bf16[384,1024]{1,0:T(8,128)(2,1)S(1)} %convolution_convert_fusion.3), channel_id=1, source_target_pairs={{0,1},{1,0},{2,3},{3,2},{4,5},{5,4},{6,7},{7,6},{8,9},{9,8},{10,11... | collective-permute-start | bytes 2359304 | tf_op jit(solution)/shard_map/ppermute | solution.py:457
  136.4 4.9 %collective-permute-start.34 = (bf16[24,768]{1,0:T(8,128)(2,1)S(1)}, bf16[24,768]{1,0:T(8,128)(2,1)S(1)}, u32[]{:S(2)}, u32[]{:S(2)}) collective-permute-start(bf16[24,768]{1,0:T(8,128)(2,1)S(1)} %slice_bitcast_fusion.68), channel_id=1, source_target_pairs={{0,16},{2,18},{4,20},{6,22},{8,24},{10,26},{12,28},{14,30},{16,0},... | collective-permute-start | bytes 110600 | tf_op jit(solution)/shard_map/ppermute | solution.py:459
  142.7 5.2 %collective-permute-start.9 = (bf16[192,384]{1,0:T(8,128)(2,1)S(1)}, bf16[192,384]{1,0:T(8,128)(2,1)S(1)}, u32[]{:S(2)}, u32[]{:S(2)}) collective-permute-start(bf16[192,384]{1,0:T(8,128)(2,1)S(1)} %slice_bitcast_fusion.28), channel_id=1, source_target_pairs={{0,2},{2,0},{4,6},{6,4},{8,10},{10,8},{12,14},{14,12},{16,18},{18,... | collective-permute-start | bytes 442376 | tf_op jit(solution)/shard_map/ppermute | solution.py:459
  143.3 32.7 %copy-start.23 = (bf16[16,96,512]{2,1,0:T(8,128)(2,1)S(1)}, bf16[16,96,512]{2,1,0:T(8,128)(2,1)}, u32[]{:S(2)}) copy-start(bf16[16,96,512]{2,1,0:T(8,128)(2,1)} %get-tuple-element.80) | copy-start | bytes 4718596
  143.3 32.7 %copy-start.25 = (bf16[1,512,768]{2,1,0:T(8,128)(2,1)S(1)}, bf16[1,512,768]{2,1,0:T(8,128)(2,1)}, u32[]{:S(2)}) copy-start(bf16[1,512,768]{2,1,0:T(8,128)(2,1)} %param.22) | copy-start | bytes 2359300
  143.4 6.5 %collective-permute-start.13 = (bf16[192,384]{1,0:T(8,128)(2,1)S(1)}, bf16[192,384]{1,0:T(8,128)(2,1)S(1)}, u32[]{:S(2)}, u32[]{:S(2)}) collective-permute-start(bf16[192,384]{1,0:T(8,128)(2,1)S(1)} %bitcast.528), channel_id=1, source_target_pairs={{0,4},{2,6},{4,0},{6,2},{8,12},{10,14},{12,8},{14,10},{16,20},{18,... | collective-permute-start | bytes 442376 | tf_op jit(solution)/shard_map/ppermute | solution.py:459
  147.9 5.1 %collective-permute-start.5 = (bf16[192,384]{1,0:T(8,128)(2,1)S(1)}, bf16[192,384]{1,0:T(8,128)(2,1)S(1)}, u32[]{:S(2)}, u32[]{:S(2)}) collective-permute-start(bf16[192,384]{1,0:T(8,128)(2,1)S(1)} %bitcast.527), channel_id=1, source_target_pairs={{0,8},{2,10},{4,12},{6,14},{8,0},{10,2},{12,4},{14,6},{16,24},{18,... | collective-permute-start | bytes 442376 | tf_op jit(solution)/shard_map/ppermute | solution.py:459
  149.9 4.4 %collective-permute-start.10 = (bf16[96,384]{1,0:T(8,128)(2,1)S(1)}, bf16[96,384]{1,0:T(8,128)(2,1)S(1)}, u32[]{:S(2)}, u32[]{:S(2)}) collective-permute-start(bf16[96,384]{1,0:T(8,128)(2,1)S(1)} %slice_bitcast_fusion.52), channel_id=1, source_target_pairs={{0,4},{2,6},{4,0},{6,2},{8,12},{10,14},{12,8},{14,10},{16,20},{18,... | collective-permute-start | bytes 221192 | tf_op jit(solution)/shard_map/ppermute | solution.py:459
  153.1 4.4 %collective-permute-start.14 = (bf16[96,384]{1,0:T(8,128)(2,1)S(1)}, bf16[96,384]{1,0:T(8,128)(2,1)S(1)}, u32[]{:S(2)}, u32[]{:S(2)}) collective-permute-start(bf16[96,384]{1,0:T(8,128)(2,1)S(1)} %slice_bitcast_fusion.50), channel_id=1, source_target_pairs={{0,2},{2,0},{4,6},{6,4},{8,10},{10,8},{12,14},{14,12},{16,18},{18,... | collective-permute-start | bytes 221192 | tf_op jit(solution)/shard_map/ppermute | solution.py:459
  154.3 5.0 %collective-permute-start.6 = (bf16[96,384]{1,0:T(8,128)(2,1)S(1)}, bf16[96,384]{1,0:T(8,128)(2,1)S(1)}, u32[]{:S(2)}, u32[]{:S(2)}) collective-permute-start(bf16[96,384]{1,0:T(8,128)(2,1)S(1)} %slice_bitcast_fusion.54), channel_id=1, source_target_pairs={{0,2},{2,0},{4,6},{6,4},{8,10},{10,8},{12,14},{14,12},{16,18},{18,... | collective-permute-start | bytes 221192 | tf_op jit(solution)/shard_map/ppermute | solution.py:459
  157.4 4.0 %collective-permute-start.11 = (bf16[48,384]{1,0:T(8,128)(2,1)S(1)}, bf16[48,384]{1,0:T(8,128)(2,1)S(1)}, u32[]{:S(2)}, u32[]{:S(2)}) collective-permute-start(bf16[48,384]{1,0:T(8,128)(2,1)S(1)} %slice_bitcast_fusion.78), channel_id=1, source_target_pairs={{0,8},{2,10},{4,12},{6,14},{8,0},{10,2},{12,4},{14,6},{16,24},{18,... | collective-permute-start | bytes 110600 | tf_op jit(solution)/shard_map/ppermute | solution.py:459
  159.4 4.2 %collective-permute-start.15 = (bf16[48,384]{1,0:T(8,128)(2,1)S(1)}, bf16[48,384]{1,0:T(8,128)(2,1)S(1)}, u32[]{:S(2)}, u32[]{:S(2)}) collective-permute-start(bf16[48,384]{1,0:T(8,128)(2,1)S(1)} %slice_bitcast_fusion.76), channel_id=1, source_target_pairs={{0,8},{2,10},{4,12},{6,14},{8,0},{10,2},{12,4},{14,6},{16,24},{18,... | collective-permute-start | bytes 110600 | tf_op jit(solution)/shard_map/ppermute | solution.py:459
  161.4 5.6 %collective-permute-start.7 = (bf16[48,384]{1,0:T(8,128)(2,1)S(1)}, bf16[48,384]{1,0:T(8,128)(2,1)S(1)}, u32[]{:S(2)}, u32[]{:S(2)}) collective-permute-start(bf16[48,384]{1,0:T(8,128)(2,1)S(1)} %slice_bitcast_fusion.80), channel_id=1, source_target_pairs={{0,4},{2,6},{4,0},{6,2},{8,12},{10,14},{12,8},{14,10},{16,20},{18,... | collective-permute-start | bytes 110600 | tf_op jit(solution)/shard_map/ppermute | solution.py:459
  163.6 5.5 %collective-permute-start.12 = (bf16[24,384]{1,0:T(8,128)(2,1)S(1)}, bf16[24,384]{1,0:T(8,128)(2,1)S(1)}, u32[]{:S(2)}, u32[]{:S(2)}) collective-permute-start(bf16[24,384]{1,0:T(8,128)(2,1)S(1)} %slice_bitcast_fusion.84), channel_id=1, source_target_pairs={{0,16},{2,18},{4,20},{6,22},{8,24},{10,26},{12,28},{14,30},{16,0},... | collective-permute-start | bytes 55304 | tf_op jit(solution)/shard_map/ppermute | solution.py:459
  167.0 8.4 %collective-permute-start.16 = (bf16[24,384]{1,0:T(8,128)(2,1)S(1)}, bf16[24,384]{1,0:T(8,128)(2,1)S(1)}, u32[]{:S(2)}, u32[]{:S(2)}) collective-permute-start(bf16[24,384]{1,0:T(8,128)(2,1)S(1)} %slice_bitcast_fusion.82), channel_id=1, source_target_pairs={{0,16},{2,18},{4,20},{6,22},{8,24},{10,26},{12,28},{14,30},{16,0},... | collective-permute-start | bytes 55304 | tf_op jit(solution)/shard_map/ppermute | solution.py:459
  169.1 4.7 %collective-permute-start.8 = (bf16[24,384]{1,0:T(8,128)(2,1)S(1)}, bf16[24,384]{1,0:T(8,128)(2,1)S(1)}, u32[]{:S(2)}, u32[]{:S(2)}) collective-permute-start(bf16[24,384]{1,0:T(8,128)(2,1)S(1)} %slice_bitcast_fusion.86), channel_id=1, source_target_pairs={{0,16},{2,18},{4,20},{6,22},{8,24},{10,26},{12,28},{14,30},{16,0},... | collective-permute-start | bytes 55304 | tf_op jit(solution)/shard_map/ppermute | solution.py:459
  179.3 12.6 %collective-permute-start.49 = (bf16[768,256]{1,0:T(8,128)(2,1)S(1)}, bf16[768,256]{1,0:T(8,128)(2,1)S(1)}, u32[]{:S(2)}, u32[]{:S(2)}) collective-permute-start(bf16[768,256]{1,0:T(8,128)(2,1)S(1)} %slice_bitcast_fusion), channel_id=1, source_target_pairs={{0,2},{2,0},{4,6},{6,4},{8,10},{10,8},{12,14},{14,12},{16,18},{18,... | collective-permute-start | bytes 1179656 | tf_op jit(solution)/shard_map/ppermute | solution.py:459
  179.8 13.5 %collective-permute-start.53 = (bf16[768,256]{1,0:T(8,128)(2,1)S(1)}, bf16[768,256]{1,0:T(8,128)(2,1)S(1)}, u32[]{:S(2)}, u32[]{:S(2)}) collective-permute-start(bf16[768,256]{1,0:T(8,128)(2,1)S(1)} %bitcast.491), channel_id=1, source_target_pairs={{0,4},{2,6},{4,0},{6,2},{8,12},{10,14},{12,8},{14,10},{16,20},{18,... | collective-permute-start | bytes 1179656 | tf_op jit(solution)/shard_map/ppermute | solution.py:459
  180.4 19.8 %collective-permute-start.57 = (bf16[768,256]{1,0:T(8,128)(2,1)S(1)}, bf16[768,256]{1,0:T(8,128)(2,1)S(1)}, u32[]{:S(2)}, u32[]{:S(2)}) collective-permute-start(bf16[768,256]{1,0:T(8,128)(2,1)S(1)} %bitcast.488), channel_id=1, source_target_pairs={{0,8},{2,10},{4,12},{6,14},{8,0},{10,2},{12,4},{14,6},{16,24},{18,... | collective-permute-start | bytes 1179656 | tf_op jit(solution)/shard_map/ppermute | solution.py:459
  185.8 12.8 %collective-permute-start.36 = (bf16[192,1024]{1,0:T(8,128)(2,1)S(1)}, bf16[192,1024]{1,0:T(8,128)(2,1)S(1)}, u32[]{:S(2)}, u32[]{:S(2)}) collective-permute-start(bf16[192,1024]{1,0:T(8,128)(2,1)S(1)} %slice_bitcast_fusion.2), channel_id=1, source_target_pairs={{0,2},{2,0},{4,6},{6,4},{8,10},{10,8},{12,14},{14,12},{16,18},{18,... | collective-permute-start | bytes 1179656 | tf_op jit(solution)/shard_map/ppermute | solution.py:459
  187.5 13.0 %collective-permute-start.40 = (bf16[192,1024]{1,0:T(8,128)(2,1)S(1)}, bf16[192,1024]{1,0:T(8,128)(2,1)S(1)}, u32[]{:S(2)}, u32[]{:S(2)}) collective-permute-start(bf16[192,1024]{1,0:T(8,128)(2,1)S(1)} %bitcast.490), channel_id=1, source_target_pairs={{0,4},{2,6},{4,0},{6,2},{8,12},{10,14},{12,8},{14,10},{16,20},{18,... | collective-permute-start | bytes 1179656 | tf_op jit(solution)/shard_map/ppermute | solution.py:459
  192.0 10.4 %collective-permute-start.44 = (bf16[192,1024]{1,0:T(8,128)(2,1)S(1)}, bf16[192,1024]{1,0:T(8,128)(2,1)S(1)}, u32[]{:S(2)}, u32[]{:S(2)}) collective-permute-start(bf16[192,1024]{1,0:T(8,128)(2,1)S(1)} %bitcast.489), channel_id=1, source_target_pairs={{0,8},{2,10},{4,12},{6,14},{8,0},{10,2},{12,4},{14,6},{16,24},{18,... | collective-permute-start | bytes 1179656 | tf_op jit(solution)/shard_map/ppermute | solution.py:459
  193.3 11.6 %collective-permute-start.18 = (bf16[192,768]{1,0:T(8,128)(2,1)S(1)}, bf16[192,768]{1,0:T(8,128)(2,1)S(1)}, u32[]{:S(2)}, u32[]{:S(2)}) collective-permute-start(bf16[192,768]{1,0:T(8,128)(2,1)S(1)} %slice_bitcast_fusion.6), channel_id=1, source_target_pairs={{0,2},{2,0},{4,6},{6,4},{8,10},{10,8},{12,14},{14,12},{16,18},{18,... | collective-permute-start | bytes 884744 | tf_op jit(solution)/shard_map/ppermute | solution.py:459
  198.6 8.9 %collective-permute-start.22 = (bf16[192,768]{1,0:T(8,128)(2,1)S(1)}, bf16[192,768]{1,0:T(8,128)(2,1)S(1)}, u32[]{:S(2)}, u32[]{:S(2)}) collective-permute-start(bf16[192,768]{1,0:T(8,128)(2,1)S(1)} %bitcast.519), channel_id=1, source_target_pairs={{0,4},{2,6},{4,0},{6,2},{8,12},{10,14},{12,8},{14,10},{16,20},{18,... | collective-permute-start | bytes 884744 | tf_op jit(solution)/shard_map/ppermute | solution.py:459
  200.2 8.9 %collective-permute-start.26 = (bf16[192,768]{1,0:T(8,128)(2,1)S(1)}, bf16[192,768]{1,0:T(8,128)(2,1)S(1)}, u32[]{:S(2)}, u32[]{:S(2)}) collective-permute-start(bf16[192,768]{1,0:T(8,128)(2,1)S(1)} %bitcast.518), channel_id=1, source_target_pairs={{0,8},{2,10},{4,12},{6,14},{8,0},{10,2},{12,4},{14,6},{16,24},{18,... | collective-permute-start | bytes 884744 | tf_op jit(solution)/shard_map/ppermute | solution.py:459
  200.5 10.0 %collective-permute-start.50 = (bf16[384,256]{1,0:T(8,128)(2,1)S(1)}, bf16[384,256]{1,0:T(8,128)(2,1)S(1)}, u32[]{:S(2)}, u32[]{:S(2)}) collective-permute-start(bf16[384,256]{1,0:T(8,128)(2,1)S(1)} %slice_bitcast_fusion.12), channel_id=1, source_target_pairs={{0,4},{2,6},{4,0},{6,2},{8,12},{10,14},{12,8},{14,10},{16,20},{18,... | collective-permute-start | bytes 589832 | tf_op jit(solution)/shard_map/ppermute | solution.py:459
  202.4 9.2 %collective-permute-start.54 = (bf16[384,256]{1,0:T(8,128)(2,1)S(1)}, bf16[384,256]{1,0:T(8,128)(2,1)S(1)}, u32[]{:S(2)}, u32[]{:S(2)}) collective-permute-start(bf16[384,256]{1,0:T(8,128)(2,1)S(1)} %slice_bitcast_fusion.10), channel_id=1, source_target_pairs={{0,2},{2,0},{4,6},{6,4},{8,10},{10,8},{12,14},{14,12},{16,18},{18,... | collective-permute-start | bytes 589832 | tf_op jit(solution)/shard_map/ppermute | solution.py:459
  204.9 9.6 %collective-permute-start.58 = (bf16[384,256]{1,0:T(8,128)(2,1)S(1)}, bf16[384,256]{1,0:T(8,128)(2,1)S(1)}, u32[]{:S(2)}, u32[]{:S(2)}) collective-permute-start(bf16[384,256]{1,0:T(8,128)(2,1)S(1)} %slice_bitcast_fusion.8), channel_id=1, source_target_pairs={{0,2},{2,0},{4,6},{6,4},{8,10},{10,8},{12,14},{14,12},{16,18},{18,... | collective-permute-start | bytes 589832 | tf_op jit(solution)/shard_map/ppermute | solution.py:459
  207.5 7.5 %collective-permute-start.37 = (bf16[96,1024]{1,0:T(8,128)(2,1)S(1)}, bf16[96,1024]{1,0:T(8,128)(2,1)S(1)}, u32[]{:S(2)}, u32[]{:S(2)}) collective-permute-start(bf16[96,1024]{1,0:T(8,128)(2,1)S(1)} %slice_bitcast_fusion.18), channel_id=1, source_target_pairs={{0,4},{2,6},{4,0},{6,2},{8,12},{10,14},{12,8},{14,10},{16,20},{18,... | collective-permute-start | bytes 589832 | tf_op jit(solution)/shard_map/ppermute | solution.py:459
  209.2 8.8 %collective-permute-start.41 = (bf16[96,1024]{1,0:T(8,128)(2,1)S(1)}, bf16[96,1024]{1,0:T(8,128)(2,1)S(1)}, u32[]{:S(2)}, u32[]{:S(2)}) collective-permute-start(bf16[96,1024]{1,0:T(8,128)(2,1)S(1)} %slice_bitcast_fusion.16), channel_id=1, source_target_pairs={{0,2},{2,0},{4,6},{6,4},{8,10},{10,8},{12,14},{14,12},{16,18},{18,... | collective-permute-start | bytes 589832 | tf_op jit(solution)/shard_map/ppermute | solution.py:459
  210.5 9.6 %collective-permute-start.45 = (bf16[96,1024]{1,0:T(8,128)(2,1)S(1)}, bf16[96,1024]{1,0:T(8,128)(2,1)S(1)}, u32[]{:S(2)}, u32[]{:S(2)}) collective-permute-start(bf16[96,1024]{1,0:T(8,128)(2,1)S(1)} %slice_bitcast_fusion.14), channel_id=1, source_target_pairs={{0,2},{2,0},{4,6},{6,4},{8,10},{10,8},{12,14},{14,12},{16,18},{18,... | collective-permute-start | bytes 589832 | tf_op jit(solution)/shard_map/ppermute | solution.py:459
  211.5 10.2 %collective-permute-start.19 = (bf16[96,768]{1,0:T(8,128)(2,1)S(1)}, bf16[96,768]{1,0:T(8,128)(2,1)S(1)}, u32[]{:S(2)}, u32[]{:S(2)}) collective-permute-start(bf16[96,768]{1,0:T(8,128)(2,1)S(1)} %slice_bitcast_fusion.26), channel_id=1, source_target_pairs={{0,4},{2,6},{4,0},{6,2},{8,12},{10,14},{12,8},{14,10},{16,20},{18,... | collective-permute-start | bytes 442376 | tf_op jit(solution)/shard_map/ppermute | solution.py:459
  214.5 7.8 %collective-permute-start.23 = (bf16[96,768]{1,0:T(8,128)(2,1)S(1)}, bf16[96,768]{1,0:T(8,128)(2,1)S(1)}, u32[]{:S(2)}, u32[]{:S(2)}) collective-permute-start(bf16[96,768]{1,0:T(8,128)(2,1)S(1)} %slice_bitcast_fusion.24), channel_id=1, source_target_pairs={{0,2},{2,0},{4,6},{6,4},{8,10},{10,8},{12,14},{14,12},{16,18},{18,... | collective-permute-start | bytes 442376 | tf_op jit(solution)/shard_map/ppermute | solution.py:459
  215.0 9.0 %collective-permute-start.27 = (bf16[96,768]{1,0:T(8,128)(2,1)S(1)}, bf16[96,768]{1,0:T(8,128)(2,1)S(1)}, u32[]{:S(2)}, u32[]{:S(2)}) collective-permute-start(bf16[96,768]{1,0:T(8,128)(2,1)S(1)} %slice_bitcast_fusion.22), channel_id=1, source_target_pairs={{0,2},{2,0},{4,6},{6,4},{8,10},{10,8},{12,14},{14,12},{16,18},{18,... | collective-permute-start | bytes 442376 | tf_op jit(solution)/shard_map/ppermute | solution.py:459
  218.0 6.8 %collective-permute-start.51 = (bf16[192,256]{1,0:T(8,128)(2,1)S(1)}, bf16[192,256]{1,0:T(8,128)(2,1)S(1)}, u32[]{:S(2)}, u32[]{:S(2)}) collective-permute-start(bf16[192,256]{1,0:T(8,128)(2,1)S(1)} %slice_bitcast_fusion.34), channel_id=1, source_target_pairs={{0,8},{2,10},{4,12},{6,14},{8,0},{10,2},{12,4},{14,6},{16,24},{18,... | collective-permute-start | bytes 294920 | tf_op jit(solution)/shard_map/ppermute | solution.py:459
  220.1 6.1 %collective-permute-start.55 = (bf16[192,256]{1,0:T(8,128)(2,1)S(1)}, bf16[192,256]{1,0:T(8,128)(2,1)S(1)}, u32[]{:S(2)}, u32[]{:S(2)}) collective-permute-start(bf16[192,256]{1,0:T(8,128)(2,1)S(1)} %slice_bitcast_fusion.32), channel_id=1, source_target_pairs={{0,8},{2,10},{4,12},{6,14},{8,0},{10,2},{12,4},{14,6},{16,24},{18,... | collective-permute-start | bytes 294920 | tf_op jit(solution)/shard_map/ppermute | solution.py:459
  221.7 5.4 %collective-permute-start.59 = (bf16[192,256]{1,0:T(8,128)(2,1)S(1)}, bf16[192,256]{1,0:T(8,128)(2,1)S(1)}, u32[]{:S(2)}, u32[]{:S(2)}) collective-permute-start(bf16[192,256]{1,0:T(8,128)(2,1)S(1)} %slice_bitcast_fusion.30), channel_id=1, source_target_pairs={{0,4},{2,6},{4,0},{6,2},{8,12},{10,14},{12,8},{14,10},{16,20},{18,... | collective-permute-start | bytes 294920 | tf_op jit(solution)/shard_map/ppermute | solution.py:459
  222.3 6.2 %collective-permute-start.38 = (bf16[48,1024]{1,0:T(8,128)(2,1)S(1)}, bf16[48,1024]{1,0:T(8,128)(2,1)S(1)}, u32[]{:S(2)}, u32[]{:S(2)}) collective-permute-start(bf16[48,1024]{1,0:T(8,128)(2,1)S(1)} %slice_bitcast_fusion.40), channel_id=1, source_target_pairs={{0,8},{2,10},{4,12},{6,14},{8,0},{10,2},{12,4},{14,6},{16,24},{18,... | collective-permute-start | bytes 294920 | tf_op jit(solution)/shard_map/ppermute | solution.py:459
  224.0 5.7 %collective-permute-start.42 = (bf16[48,1024]{1,0:T(8,128)(2,1)S(1)}, bf16[48,1024]{1,0:T(8,128)(2,1)S(1)}, u32[]{:S(2)}, u32[]{:S(2)}) collective-permute-start(bf16[48,1024]{1,0:T(8,128)(2,1)S(1)} %slice_bitcast_fusion.38), channel_id=1, source_target_pairs={{0,8},{2,10},{4,12},{6,14},{8,0},{10,2},{12,4},{14,6},{16,24},{18,... | collective-permute-start | bytes 294920 | tf_op jit(solution)/shard_map/ppermute | solution.py:459
  224.8 7.3 %collective-permute-start.46 = (bf16[48,1024]{1,0:T(8,128)(2,1)S(1)}, bf16[48,1024]{1,0:T(8,128)(2,1)S(1)}, u32[]{:S(2)}, u32[]{:S(2)}) collective-permute-start(bf16[48,1024]{1,0:T(8,128)(2,1)S(1)} %slice_bitcast_fusion.36), channel_id=1, source_target_pairs={{0,4},{2,6},{4,0},{6,2},{8,12},{10,14},{12,8},{14,10},{16,20},{18,... | collective-permute-start | bytes 294920 | tf_op jit(solution)/shard_map/ppermute | solution.py:459
  226.3 6.6 %collective-permute-start.20 = (bf16[48,768]{1,0:T(8,128)(2,1)S(1)}, bf16[48,768]{1,0:T(8,128)(2,1)S(1)}, u32[]{:S(2)}, u32[]{:S(2)}) collective-permute-start(bf16[48,768]{1,0:T(8,128)(2,1)S(1)} %slice_bitcast_fusion.48), channel_id=1, source_target_pairs={{0,8},{2,10},{4,12},{6,14},{8,0},{10,2},{12,4},{14,6},{16,24},{18,... | collective-permute-start | bytes 221192 | tf_op jit(solution)/shard_map/ppermute | solution.py:459
  227.1 8.2 %collective-permute-start.24 = (bf16[48,768]{1,0:T(8,128)(2,1)S(1)}, bf16[48,768]{1,0:T(8,128)(2,1)S(1)}, u32[]{:S(2)}, u32[]{:S(2)}) collective-permute-start(bf16[48,768]{1,0:T(8,128)(2,1)S(1)} %slice_bitcast_fusion.46), channel_id=1, source_target_pairs={{0,8},{2,10},{4,12},{6,14},{8,0},{10,2},{12,4},{14,6},{16,24},{18,... | collective-permute-start | bytes 221192 | tf_op jit(solution)/shard_map/ppermute | solution.py:459
  228.5 7.4 %collective-permute-start.28 = (bf16[48,768]{1,0:T(8,128)(2,1)S(1)}, bf16[48,768]{1,0:T(8,128)(2,1)S(1)}, u32[]{:S(2)}, u32[]{:S(2)}) collective-permute-start(bf16[48,768]{1,0:T(8,128)(2,1)S(1)} %slice_bitcast_fusion.44), channel_id=1, source_target_pairs={{0,4},{2,6},{4,0},{6,2},{8,12},{10,14},{12,8},{14,10},{16,20},{18,... | collective-permute-start | bytes 221192 | tf_op jit(solution)/shard_map/ppermute | solution.py:459
  229.7 17.1 %collective-permute-start.52 = (bf16[96,256]{1,0:T(8,128)(2,1)S(1)}, bf16[96,256]{1,0:T(8,128)(2,1)S(1)}, u32[]{:S(2)}, u32[]{:S(2)}) collective-permute-start(bf16[96,256]{1,0:T(8,128)(2,1)S(1)} %slice_bitcast_fusion.60), channel_id=1, source_target_pairs={{0,16},{2,18},{4,20},{6,22},{8,24},{10,26},{12,28},{14,30},{16,0},... | collective-permute-start | bytes 147464 | tf_op jit(solution)/shard_map/ppermute | solution.py:459
  232.2 17.4 %collective-permute-start.56 = (bf16[96,256]{1,0:T(8,128)(2,1)S(1)}, bf16[96,256]{1,0:T(8,128)(2,1)S(1)}, u32[]{:S(2)}, u32[]{:S(2)}) collective-permute-start(bf16[96,256]{1,0:T(8,128)(2,1)S(1)} %slice_bitcast_fusion.58), channel_id=1, source_target_pairs={{0,16},{2,18},{4,20},{6,22},{8,24},{10,26},{12,28},{14,30},{16,0},... | collective-permute-start | bytes 147464 | tf_op jit(solution)/shard_map/ppermute | solution.py:459
  232.8 16.8 %collective-permute-start.60 = (bf16[96,256]{1,0:T(8,128)(2,1)S(1)}, bf16[96,256]{1,0:T(8,128)(2,1)S(1)}, u32[]{:S(2)}, u32[]{:S(2)}) collective-permute-start(bf16[96,256]{1,0:T(8,128)(2,1)S(1)} %slice_bitcast_fusion.56), channel_id=1, source_target_pairs={{0,16},{2,18},{4,20},{6,22},{8,24},{10,26},{12,28},{14,30},{16,0},... | collective-permute-start | bytes 147464 | tf_op jit(solution)/shard_map/ppermute | solution.py:459
  235.3 5.6 %collective-permute-start.39 = (bf16[24,1024]{1,0:T(8,128)(2,1)S(1)}, bf16[24,1024]{1,0:T(8,128)(2,1)S(1)}, u32[]{:S(2)}, u32[]{:S(2)}) collective-permute-start(bf16[24,1024]{1,0:T(8,128)(2,1)S(1)} %slice_bitcast_fusion.66), channel_id=1, source_target_pairs={{0,16},{2,18},{4,20},{6,22},{8,24},{10,26},{12,28},{14,30},{16,0},... | collective-permute-start | bytes 147464 | tf_op jit(solution)/shard_map/ppermute | solution.py:459
  236.0 7.0 %collective-permute-start.43 = (bf16[24,1024]{1,0:T(8,128)(2,1)S(1)}, bf16[24,1024]{1,0:T(8,128)(2,1)S(1)}, u32[]{:S(2)}, u32[]{:S(2)}) collective-permute-start(bf16[24,1024]{1,0:T(8,128)(2,1)S(1)} %slice_bitcast_fusion.64), channel_id=1, source_target_pairs={{0,16},{2,18},{4,20},{6,22},{8,24},{10,26},{12,28},{14,30},{16,0},... | collective-permute-start | bytes 147464 | tf_op jit(solution)/shard_map/ppermute | solution.py:459
  240.9 5.0 %collective-permute-start.47 = (bf16[24,1024]{1,0:T(8,128)(2,1)S(1)}, bf16[24,1024]{1,0:T(8,128)(2,1)S(1)}, u32[]{:S(2)}, u32[]{:S(2)}) collective-permute-start(bf16[24,1024]{1,0:T(8,128)(2,1)S(1)} %slice_bitcast_fusion.62), channel_id=1, source_target_pairs={{0,16},{2,18},{4,20},{6,22},{8,24},{10,26},{12,28},{14,30},{16,0},... | collective-permute-start | bytes 147464 | tf_op jit(solution)/shard_map/ppermute | solution.py:459
  243.0 7.4 %collective-permute-start.21 = (bf16[24,768]{1,0:T(8,128)(2,1)S(1)}, bf16[24,768]{1,0:T(8,128)(2,1)S(1)}, u32[]{:S(2)}, u32[]{:S(2)}) collective-permute-start(bf16[24,768]{1,0:T(8,128)(2,1)S(1)} %slice_bitcast_fusion.74), channel_id=1, source_target_pairs={{0,16},{2,18},{4,20},{6,22},{8,24},{10,26},{12,28},{14,30},{16,0},... | collective-permute-start | bytes 110600 | tf_op jit(solution)/shard_map/ppermute | solution.py:459
  245.9 4.9 %collective-permute-start.25 = (bf16[24,768]{1,0:T(8,128)(2,1)S(1)}, bf16[24,768]{1,0:T(8,128)(2,1)S(1)}, u32[]{:S(2)}, u32[]{:S(2)}) collective-permute-start(bf16[24,768]{1,0:T(8,128)(2,1)S(1)} %slice_bitcast_fusion.72), channel_id=1, source_target_pairs={{0,16},{2,18},{4,20},{6,22},{8,24},{10,26},{12,28},{14,30},{16,0},... | collective-permute-start | bytes 110600 | tf_op jit(solution)/shard_map/ppermute | solution.py:459
  246.7 4.9 %collective-permute-start.29 = (bf16[24,768]{1,0:T(8,128)(2,1)S(1)}, bf16[24,768]{1,0:T(8,128)(2,1)S(1)}, u32[]{:S(2)}, u32[]{:S(2)}) collective-permute-start(bf16[24,768]{1,0:T(8,128)(2,1)S(1)} %slice_bitcast_fusion.70), channel_id=1, source_target_pairs={{0,16},{2,18},{4,20},{6,22},{8,24},{10,26},{12,28},{14,30},{16,0},... | collective-permute-start | bytes 110600 | tf_op jit(solution)/shard_map/ppermute | solution.py:459
  (36 other events, 204.0 us)
